TPU v7x, 128 devices: a whole 4x4x4 slice. The times are simulated.
128 devices in a mesh: seq: 32 (over x, z, core), head: 4 (over y).
Axes of the slice: x: 4, y: 4, z: 4, core: 2. Of those that a mesh axis runs over, the one named last changes fastest.
Arguments:
- tokens: bfloat16 [16384, 4096], P('seq', 'head'), may hold values from -80 to 80, as said below
- w_query: bfloat16 [4096, 2048], P(None, 'head'), may hold values from -0.09375 to 0.09375
- w_key: bfloat16 [4096, 2048], P(None, 'head'), may hold values from -0.09375 to 0.09375
- w_value: bfloat16 [4096, 2048], P(None, 'head'), may hold values from -0.09375 to 0.09375
- w_out: bfloat16 [2048, 4096], P('head'), may hold values from -0.125 to 0.125
- block_bucket: int32 [128], P('seq'), may hold values from 0 to 575, as said below
Outputs:
- attended: bfloat16 [16384, 4096], P('seq', 'head')
Inputs may be any that keep to these rules, and one draw needn't show every extreme that they name: `tokens`: hidden states of order one; a few rows may be far larger. `block_bucket`: no bucket holds more than 2 blocks, and some bucket holds exactly 2; an owner's buckets are numbered from its first id on and hold 2 blocks each except possibly its first and its last. The blocks of one index of seq belong to buckets of at most 1 block per owner, and some owner receives exactly 1 from every index of seq.
All inputs are finite; a program needn't handle non-finite values.
Results may differ from a plain program's by a relative error of at most 0.012.
The roundings to bfloat16 on the way count: a program that leaves them out, or rounds other values in their place, can miss the bound.
Values may be sent and summed in bfloat16 or wider, within the bound.
A program may use at most 128 MiB of HBM per device.

v0:
```python
import jax
import jax.numpy as jnp
from jax import lax
from jax.sharding import PartitionSpec as P

HDIM = 128
BMAX = 2


def in_blocks(array, dim, count):
    before, after = (array.shape[:dim], array.shape[dim + 1 :])
    return jnp.moveaxis(array.reshape(*before, count, -1, *after), dim, 0)


def piece_ends(length, count):
    turn = length // count
    if turn >= 8:
        turn -= turn % 8
    return [turn * k for k in range(1, count)]


def laid_out(blocks, dim):
    blocks = jnp.moveaxis(blocks, 0, dim)
    shape = blocks.shape
    return blocks.reshape(*shape[:dim], shape[dim] * shape[dim + 1], *shape[dim + 2 :])


def exchange_in_pieces(array, axis, pieces, split_dim, concat_dim):
    blocks = in_blocks(array, split_dim, lax.axis_size(axis))
    cut = max(range(1, max(2, blocks.ndim - 1)), key=lambda d: blocks.shape[d])
    finished = []
    for share in jnp.split(blocks, piece_ends(blocks.shape[cut], pieces), axis=cut):
        if share.size:
            finished.append(lax.all_to_all(share, axis, split_axis=0, concat_axis=0, tiled=True))
    return laid_out(jnp.concatenate(finished, axis=cut), concat_dim)


def key_lists(bucket, valid):
    count = bucket.shape[0]
    match = (bucket[:, None] == bucket[None, :]) & valid[None, :]
    rank = jnp.cumsum(match.astype(jnp.int32), axis=1) - 1
    picks = match[:, :, None] & (
        rank[:, :, None] == jnp.arange(BMAX, dtype=jnp.int32)[None, None, :]
    )
    places = jnp.arange(count, dtype=jnp.int32)[None, :, None]
    index = jnp.sum(jnp.where(picks, places, 0), axis=1)
    usable = jnp.any(picks, axis=1)
    return (index, usable)


def per_device(tokens, w_query, w_key, w_value, w_out, block_bucket):
    seq_count = lax.axis_size("seq")
    head_count = lax.axis_size("head")
    blocks_here = block_bucket.shape[0]
    tok_here = tokens.shape[0]
    block_len = tok_here // blocks_here
    capacity = (blocks_here + seq_count - 1) // seq_count
    slot_count = seq_count * capacity
    local_width = w_query.shape[1]
    heads_here = local_width // HDIM
    owned = seq_count * capacity // BMAX + 2
    piece = lax.all_gather(tokens, "head", axis=1, tiled=True)
    query, keys, values = tuple(
        (
            jnp.dot(piece, weight, preferred_element_type=jnp.float32)
            for weight in (w_query, w_key, w_value)
        )
    )
    packed = jnp.concatenate(
        [query.astype(jnp.bfloat16), keys.astype(jnp.bfloat16), values.astype(jnp.bfloat16)], axis=1
    )
    packed = packed.reshape(blocks_here, block_len, 3 * local_width)
    owner = block_bucket // owned
    places = jnp.arange(blocks_here, dtype=jnp.int32)
    earlier = (owner[:, None] == owner[None, :]) & (places[None, :] < places[:, None])
    rank = jnp.sum(earlier.astype(jnp.int32), axis=1)
    slot_of_block = owner * capacity + rank
    hits = slot_of_block[None, :] == jnp.arange(slot_count, dtype=jnp.int32)[:, None]
    source_index = jnp.sum(jnp.where(hits, places[None, :], 0), axis=1)
    filled = jnp.any(hits, axis=1)
    outgoing = jnp.take(packed, source_index, axis=0)
    outgoing_ids = jnp.where(filled, jnp.take(block_bucket, source_index), -1)
    arrived, arrived_ids = (
        exchange_in_pieces(outgoing, "seq", 2, 0, 0),
        exchange_in_pieces(outgoing_ids, "seq", 2, 0, 0),
    )
    index, usable = key_lists(arrived_ids, arrived_ids >= 0)
    mask = jnp.repeat(usable, block_len, axis=1)

    def head_attend(which):
        query_head = lax.dynamic_slice_in_dim(arrived, which * HDIM, HDIM, 2)
        key_head = lax.dynamic_slice_in_dim(arrived, local_width + which * HDIM, HDIM, 2)
        value_head = lax.dynamic_slice_in_dim(arrived, 2 * local_width + which * HDIM, HDIM, 2)
        key_rows = jnp.take(key_head, index, axis=0).reshape(slot_count, BMAX * block_len, HDIM)
        value_rows = jnp.take(value_head, index, axis=0).reshape(slot_count, BMAX * block_len, HDIM)
        scores = jnp.einsum(
            "sqd,skd->sqk", query_head, key_rows, preferred_element_type=jnp.float32
        ) * HDIM ** (-0.5)
        scores = jnp.where(mask[:, None, :], scores, -1e30)
        top = jnp.max(scores, axis=-1, keepdims=True)
        expo = jnp.exp(scores - top)
        weights = (expo / jnp.sum(expo, axis=-1, keepdims=True)).astype(jnp.bfloat16)
        mixed = jnp.einsum("sqk,skd->sqd", weights, value_rows, preferred_element_type=jnp.float32)
        return mixed.astype(jnp.bfloat16)

    per_head = lax.map(head_attend, jnp.arange(heads_here, dtype=jnp.int32))
    results = jnp.transpose(per_head, (1, 2, 0, 3)).reshape(slot_count, block_len, local_width)
    returned = lax.all_to_all(results, "seq", split_axis=0, concat_axis=0, tiled=True)
    mixed_here = jnp.take(returned, slot_of_block, axis=0).reshape(tok_here, local_width)
    column_width = w_out.shape[1] // head_count
    rows_split = w_out.reshape(local_width, head_count, column_width)
    columns = lax.all_to_all(rows_split, "head", split_axis=1, concat_axis=0, tiled=True)
    columns = columns.reshape(head_count * local_width, column_width)
    summed = jnp.dot(
        lax.all_gather(mixed_here, "head", axis=1, tiled=True),
        columns,
        preferred_element_type=jnp.float32,
    )
    return summed.astype(jnp.bfloat16)


def solution(mesh):
    placed = (
        P("seq", "head"),
        P(None, "head"),
        P(None, "head"),
        P(None, "head"),
        P("head", None),
        P("seq"),
    )
    return jax.shard_map(
        per_device, mesh=mesh, in_specs=placed, out_specs=P("seq", "head"), check_vma=False
    )
```

profile of v0, /device:TPU:1, one launch (start us, length us, event | category | flops | bytes accessed | tf_op | source)
XLA Modules:
  0.0 513.4 jit_solution(11713508505914483083)
XLA Ops:
  6.5 0.7 all-gather.3.cloned.1.call-update
  7.3 1.5 fusion.23
  8.7 0.7 and_select_fusion.1
  9.6 0.7 compare_and_fusion.3
  10.4 2.5 bitcast_select_fusion.2
  12.9 0.7 copy.33
  13.6 9.4 %all-to-all-start = ((s32[32,1,1]{2,1,0:T(1,128)}), s32[32,1,1]{2,1,0:T(1,128)S(1)}, u32[]{:S(2)}, u32[]{:S(2)}) async-start(s32[32,1,1]{2,1,0:T(1,128)} %copy.33), calls=%async_computation | async-start | bytes 32768 | tf_op jit(solution)/shard_map/all_to_all | solution.py:34
  23.1 37.4 %all-gather.3.cloned.1.call-done = bf16[512,4096]{1,0:T(8,128)(2,1)} async-done(((bf16[512,1024]{1,0:T(8,128)(2,1)}), bf16[512,4096]{1,0:T(8,128)(2,1)}) %all-gather.3.cloned.1.call-update) | async-done | bytes 4194320 | tf_op jit(solution)/shard_map/all_gather | solution.py:62
  60.5 6.0 %convolution_convert_fusion.1 = bf16[512,512]{0,1:T(8,128)(2,1)S(1)} fusion(bf16[512,4096]{1,0:T(8,128)(2,1)} %all-gather.3.cloned.1.call-done, bf16[4096,512]{1,0:T(8,128)(2,1)} %param.13), kind=kOutput, calls=%fused_computation.36 | convolution fusion | flops 2147745792 | bytes 8912896 | tf_op jit(solution)/shard_map/dot_general | solution.py:65
  66.5 2.4 convolution_convert_fusion.2
  68.9 2.4 convolution_convert_fusion.3
  71.4 0.7 copy.40
  72.1 6.4 %gather_fusion.2 = bf16[32,128,1536]{2,1,0:T(8,128)(2,1)} fusion(bf16[4,128,1536]{2,1,0:T(8,128)(2,1)S(1)} %bitcast.85, s32[1024]{0:T(1024)S(1)} %pad_clamp_fusion.2), kind=kCustom, calls=%fused_computation.2 | custom fusion | bytes 25165952 | tf_op jit(solution)/shard_map/jit(_take)/gather | solution.py:81
  78.5 6.5 %bitcast_select_fusion = bf16[32,1,128,1536]{3,2,0,1:T(8,128)(2,1)S(1)} fusion(bf16[32,128,1536]{2,1,0:T(8,128)(2,1)} %gather_fusion.2, pred[32]{0:T(512)(128)(4,1)S(1)} %compare_and_fusion.2), kind=kLoop, calls=%fused_computation.31 | loop fusion | flops 6291456 | bytes 25165856 | tf_op jit(solution)/shard_map/jit(_take)/select_n | solution.py:81
  85.1 4.9 slice_bitcast_fusion.1
  90.0 80.9 %all_to_all.36 = bf16[32,1,64,1536]{3,2,1,0:T(8,128)(2,1)} all-to-all(bf16[32,1,64,1536]{3,2,1,0:T(8,128)(2,1)} %get-tuple-element.126), channel_id=1, replica_groups=mesh['seq'=32,'head'=4] {'seq'}, dimensions={0} | all-to-all | bytes 12582912 | tf_op jit(solution)/shard_map/all_to_all | solution.py:34
  170.9 4.9 all-to-all-start.2
  177.2 76.0 %all-to-all-done.2 = bf16[32,1,64,1536]{3,2,1,0:T(8,128)(2,1)} async-done(((bf16[32,1,64,1536]{3,2,1,0:T(8,128)(2,1)}), bf16[32,1,64,1536]{3,2,1,0:T(8,128)(2,1)}, u32[]{:S(2)}, u32[]{:S(2)}) %all-to-all-start.2) | async-done | bytes 6291488 | tf_op jit(solution)/shard_map/all_to_all | solution.py:34
  253.2 10.6 %maximum_bitcast_fusion = bf16[32,128,1536]{2,1,0:T(8,128)(2,1)} fusion(bf16[32,1,64,1536]{3,2,1,0:T(8,128)(2,1)} %all-to-all-done.2, bf16[32,1,64,1536]{3,2,1,0:T(8,128)(2,1)} %all_to_all.36), kind=kLoop, calls=%fused_computation.30 | loop fusion | flops 25165824 | bytes 25165824 | tf_op jit(solution)/shard_map/reshape | solution.py:25
  263.8 94.5 %while.13 = (s32[]{:T(128)}, bf16[4,32,128,128]{2,3,0,1:T(8,128)(2,1)}, s32[4]{0:T(128)S(1)}, bf16[32,128,1536]{2,1,0:T(8,128)(2,1)}, s32[32,2]{1,0:T(8,128)S(1)...) while((s32[]{:T(128)}, ...), condition=%wide.region_9.11_spmd.clone, body=%wide.region_6.10_spmd.clone.sunk | while | flops 547882816 | bytes 65084444 | solution.py:106
  265.0 1.7 constant_dynamic-slice_fusion.3
  266.9 2.1 gather_fusion
  269.0 2.2 gather_fusion.1
  271.2 4.0 broadcast_select_fusion.3
  275.2 2.6 fusion.43
  278.0 6.5 %fusion.44 = (f32[32,128]{1,0:T(8,128)S(1)}, f32[32,128,256]{2,1,0:T(8,128)S(1)}) fusion(f32[32,128,256]{2,1,0:T(8,128)S(1)} %fusion.43, pred[32,256]{1,0:T(8,128)(4,1)S(1)} %bitcast.91), kind=kOutput, calls=%fused_computation.71.clone.1 | output fusion | flops 6291711 | bytes 8413184 | tf_op jit(solution)/shard_map/while/body/eval_jaxpr/sub | solution.py:101
  284.5 1.1 fusion.45
  285.5 0.7 copy.49
  286.2 1.2 constant_dynamic-update-slice_fusion.2
  288.7 1.7 constant_dynamic-slice_fusion.3
  290.5 2.1 gather_fusion
  292.7 2.2 gather_fusion.1
  294.8 4.0 broadcast_select_fusion.3
  298.8 2.6 fusion.43
  301.6 6.5 %fusion.44 = (f32[32,128]{1,0:T(8,128)S(1)}, f32[32,128,256]{2,1,0:T(8,128)S(1)}) fusion(f32[32,128,256]{2,1,0:T(8,128)S(1)} %fusion.43, pred[32,256]{1,0:T(8,128)(4,1)S(1)} %bitcast.91), kind=kOutput, calls=%fused_computation.71.clone.1 | output fusion | flops 6291711 | bytes 8413184 | tf_op jit(solution)/shard_map/while/body/eval_jaxpr/sub | solution.py:101
  308.1 1.1 fusion.45
  309.2 0.7 copy.49
  309.9 1.2 constant_dynamic-update-slice_fusion.2
  312.3 1.7 constant_dynamic-slice_fusion.3
  314.2 2.1 gather_fusion
  316.3 2.2 gather_fusion.1
  318.5 4.0 broadcast_select_fusion.3
  322.5 2.6 fusion.43
  325.3 6.5 %fusion.44 = (f32[32,128]{1,0:T(8,128)S(1)}, f32[32,128,256]{2,1,0:T(8,128)S(1)}) fusion(f32[32,128,256]{2,1,0:T(8,128)S(1)} %fusion.43, pred[32,256]{1,0:T(8,128)(4,1)S(1)} %bitcast.91), kind=kOutput, calls=%fused_computation.71.clone.1 | output fusion | flops 6291711 | bytes 8413184 | tf_op jit(solution)/shard_map/while/body/eval_jaxpr/sub | solution.py:101
  331.8 1.1 fusion.45
  332.8 0.7 copy.49
  333.5 1.2 constant_dynamic-update-slice_fusion.2
  335.9 1.7 constant_dynamic-slice_fusion.3
  337.8 2.1 gather_fusion
  339.9 2.2 gather_fusion.1
  342.1 4.0 broadcast_select_fusion.3
  346.1 2.6 fusion.43
  348.9 6.5 %fusion.44 = (f32[32,128]{1,0:T(8,128)S(1)}, f32[32,128,256]{2,1,0:T(8,128)S(1)}) fusion(f32[32,128,256]{2,1,0:T(8,128)S(1)} %fusion.43, pred[32,256]{1,0:T(8,128)(4,1)S(1)} %bitcast.91), kind=kOutput, calls=%fused_computation.71.clone.1 | output fusion | flops 6291711 | bytes 8413184 | tf_op jit(solution)/shard_map/while/body/eval_jaxpr/sub | solution.py:101
  355.4 1.1 fusion.45
  357.1 1.2 constant_dynamic-update-slice_fusion.2
  358.4 13.7 %all-to-all-start.3 = ((bf16[32,128,512]{1,2,0:T(8,128)(2,1)}), bf16[32,128,512]{1,2,0:T(8,128)(2,1)}, u32[]{:S(2)}, u32[]{:S(2)}) async-start(bf16[32,128,512]{1,2,0:T(8,128)(2,1)} %bitcast.88), calls=%async_computation.3 | async-start | bytes 8388608 | tf_op jit(solution)/shard_map/all_to_all | solution.py:108
  372.1 6.5 %copy.38 = bf16[512,4096]{0,1:T(8,128)(2,1)} copy(bf16[512,4096]{1,0:T(8,128)(2,1)} %param.14) | data formatting | bytes 8388608 | tf_op args[4]
  378.7 45.6 %all-to-all-done.3 = bf16[32,128,512]{1,2,0:T(8,128)(2,1)} async-done(((bf16[32,128,512]{1,2,0:T(8,128)(2,1)}), bf16[32,128,512]{1,2,0:T(8,128)(2,1)}, u32[]{:S(2)}, u32[]{:S(2)}) %all-to-all-start.3) | async-done | bytes 4194336 | tf_op jit(solution)/shard_map/all_to_all | solution.py:108
  424.3 4.9 all-to-all-start.4
  429.2 2.8 gather_fusion.3
  432.2 0.9 bitcast_select_fusion.1
  433.2 60.9 %all-to-all-done.4 = bf16[512,4,1024]{0,2,1:T(8,128)(2,1)} async-done(((bf16[512,4,1024]{0,2,1:T(8,128)(2,1)}), bf16[512,4,1024]{0,2,1:T(8,128)(2,1)}, u32[]{:S(2)}, u32[]{:S(2)}) %all-to-all-start.4) | async-done | bytes 4194336 | tf_op jit(solution)/shard_map/all_to_all | solution.py:112
  494.1 6.3 %copy.39 = bf16[4,512,1,1024]{3,1,0,2:T(8,128)(2,1)} copy(bf16[4,512,1,1024]{1,3,0,2:T(8,128)(2,1)} %bitcast.20) | data formatting | bytes 8388608 | tf_op jit(solution)/shard_map/all_to_all | solution.py:112
  500.4 6.1 %convolution_convert_fusion = bf16[512,1024]{1,0:T(8,128)(2,1)} fusion(bf16[512,2048]{1,0:T(8,128)(2,1)} %all-gather.5.cloned.1.call-done, bf16[2048,1024]{1,0:T(8,128)(2,1)} %bitcast.89), kind=kOutput, calls=%fused_computation.35 | convolution fusion | flops 2148007936 | bytes 7340032 | tf_op jit(solution)/shard_map/dot_general | solution.py:114
  (78 shorter events, 6.2 us)
Async XLA Ops:
  6.5 54.0 %all-gather.3.cloned.1.call-start = ((), (), s32[]{:S(2)}) async-start(), calls=%async_computation.5 | async-start | bytes 5242880 | tf_op jit(solution)/shard_map/all_gather | solution.py:62
  13.6 76.4 %all-to-all-start = ((s32[32,1,1]{2,1,0:T(1,128)}), s32[32,1,1]{2,1,0:T(1,128)S(1)}, u32[]{:S(2)}, u32[]{:S(2)}) async-start(s32[32,1,1]{2,1,0:T(1,128)} %copy.33), calls=%async_computation | async-start | bytes 32768 | tf_op jit(solution)/shard_map/all_to_all | solution.py:34
  60.5 6.0 %copy-start.2 = (bf16[4096,512]{1,0:T(8,128)(2,1)S(1)}, bf16[4096,512]{1,0:T(8,128)(2,1)}, u32[]{:S(2)}) copy-start(bf16[4096,512]{1,0:T(8,128)(2,1)} %param.12) | copy-start | bytes 12582916
  60.5 6.0 %copy-start.4 = (bf16[512,4096]{1,0:T(8,128)(2,1)S(1)}, bf16[512,4096]{1,0:T(8,128)(2,1)}, u32[]{:S(2)}) copy-start(bf16[512,4096]{1,0:T(8,128)(2,1)} %all-gather.3.cloned.1.call-done) | copy-start | bytes 12582916
  66.5 2.4 copy-start.3
  170.9 82.3 %all-to-all-start.2 = ((bf16[32,1,64,1536]{3,2,1,0:T(8,128)(2,1)}), bf16[32,1,64,1536]{3,2,1,0:T(8,128)(2,1)}, u32[]{:S(2)}, u32[]{:S(2)}) async-start(bf16[32,1,64,1536]{3,2,1,0:T(8,128)(2,1)} %get-tuple-element.127), calls=%async_computation.2 | async-start | bytes 12582912 | tf_op jit(solution)/shard_map/all_to_all | solution.py:34
  269.0 2.2 copy-start
  278.0 6.5 %copy-start.1 = (bf16[32,2,128,128]{3,2,1,0:T(8,128)(2,1)S(1)}, bf16[32,2,128,128]{3,2,1,0:T(8,128)(2,1)}, u32[]{:S(2)}) copy-start(bf16[32,2,128,128]{3,2,1,0:T(8,128)(2,1)} %get-tuple-element.179) | copy-start | bytes 6291460 | tf_op jit(solution)/shard_map/while
  292.7 2.2 copy-start
  301.6 6.5 %copy-start.1 = (bf16[32,2,128,128]{3,2,1,0:T(8,128)(2,1)S(1)}, bf16[32,2,128,128]{3,2,1,0:T(8,128)(2,1)}, u32[]{:S(2)}) copy-start(bf16[32,2,128,128]{3,2,1,0:T(8,128)(2,1)} %get-tuple-element.179) | copy-start | bytes 6291460 | tf_op jit(solution)/shard_map/while
  316.3 2.2 copy-start
  325.2 6.5 %copy-start.1 = (bf16[32,2,128,128]{3,2,1,0:T(8,128)(2,1)S(1)}, bf16[32,2,128,128]{3,2,1,0:T(8,128)(2,1)}, u32[]{:S(2)}) copy-start(bf16[32,2,128,128]{3,2,1,0:T(8,128)(2,1)} %get-tuple-element.179) | copy-start | bytes 6291460 | tf_op jit(solution)/shard_map/while
  339.9 2.2 copy-start
  348.9 6.5 %copy-start.1 = (bf16[32,2,128,128]{3,2,1,0:T(8,128)(2,1)S(1)}, bf16[32,2,128,128]{3,2,1,0:T(8,128)(2,1)}, u32[]{:S(2)}) copy-start(bf16[32,2,128,128]{3,2,1,0:T(8,128)(2,1)} %get-tuple-element.179) | copy-start | bytes 6291460 | tf_op jit(solution)/shard_map/while
  358.4 65.9 %all-to-all-start.3 = ((bf16[32,128,512]{1,2,0:T(8,128)(2,1)}), bf16[32,128,512]{1,2,0:T(8,128)(2,1)}, u32[]{:S(2)}, u32[]{:S(2)}) async-start(bf16[32,128,512]{1,2,0:T(8,128)(2,1)} %bitcast.88), calls=%async_computation.3 | async-start | bytes 8388608 | tf_op jit(solution)/shard_map/all_to_all | solution.py:108
  424.3 69.8 %all-to-all-start.4 = ((bf16[512,4,1024]{0,2,1:T(8,128)(2,1)}), bf16[512,4,1024]{0,2,1:T(8,128)(2,1)}, u32[]{:S(2)}, u32[]{:S(2)}) async-start(bf16[512,4,1024]{0,2,1:T(8,128)(2,1)} %bitcast.87), calls=%async_computation.4 | async-start | bytes 8388608 | tf_op jit(solution)/shard_map/all_to_all | solution.py:112
  429.1 71.3 %all-gather.5.cloned.1.call-start = ((), (), s32[]{:S(2)}) async-start(), calls=%async_computation.6 | async-start | bytes 2621440 | tf_op jit(solution)/shard_map/all_gather | solution.py:115
Sparse Core Ops, SparseCore 0:
  9.0 51.4 all-gather.2
  433.3 48.8 all-gather.4
where the time goes:
time: 515 us; the launch traced here: 513 us
  waiting for transfers between devices  221 us (43%)
  blocking collectives  80.9 us (16%)
  other arithmetic  65.6 us (13%)
  local copies, waits for them, and re-layouts  65.2 us (13%)
  starting transfers between devices  32.9 us (6%)
  matrix products  31.7 us (6%)
  between operations  13.6 us (3%)
    all_to_all x1, blocking collectives, exchange_in_pieces(): lax.all_to_all(share, axis, split_axis=0, concat_axis=0, tiled=True)  80.9 us
    all_to_all x2, waiting for transfers between devices, exchange_in_pieces(): lax.all_to_all(share, axis, split_axis=0, concat_axis=0, tiled=True)  76 us
    all_to_all x1, waiting for transfers between devices, per_device(): lax.all_to_all(rows_split, 'head', split_axis=1, concat_axis=0, tiled=True)  60.9 us
    all_to_all x1, waiting for transfers between devices, per_device(): lax.all_to_all(results, 'seq', split_axis=0, concat_axis=0, tiled=True)  45.6 us
    all_gather x1, waiting for transfers between devices, per_device(): piece = lax.all_gather(tokens, 'head', axis=1, tiled=True)  37.4 us
    sub x4, other arithmetic, head_attend(): expo = jnp.exp(scores - top)  25.9 us
    select_n x8, other arithmetic, head_attend(): jnp.take(key_head, index, axis=0)  16 us
    all_to_all x2, starting transfers between devices, exchange_in_pieces(): lax.all_to_all(share, axis, split_axis=0, concat_axis=0, tiled=True)  14.3 us
  transfers between devices with their start and end apart: 6, of which 4 were waited for; matrix products, arithmetic and copies ran while one was open for 11% of the time, Pallas kernels for 0%

commit v1 on v0

v1 whole, which is shorter than its diff:
```python
import jax
import jax.numpy as jnp
from jax import lax
from jax.experimental import pallas as pl
from jax.experimental.pallas import tpu as pltpu
from jax.sharding import PartitionSpec as P

HDIM = 128
SCALE = HDIM ** (-0.5)
BLK = 128
HALF = BLK // 2
NB = 4
FEAT = 1024
WIDTH = 512
PACK = 512
MESH = pl.DeviceIdType.MESH
F32 = jnp.float32
BF16 = jnp.bfloat16


def wrap(n):
    return lax.rem(n + 4, 4)


def kernel(
    ids, tok, wq, wk, wv, wo, out,
    tk, w, acc, qs, s1a, s1b, tx, rel, fin, kvp, wov, wrel, mx,
    idg, idsend, part_v, part_s,
    loc_sem, wloc_sem, tok_s, tok_r, id_s, id_r, ag_s, ag_r, rs_s, rs_r, wo_s, wo_r, mx_s, mx_r,
):
    s = lax.axis_index("seq")
    y = lax.axis_index("head")
    x = s // 8
    z = lax.rem(s // 2, 4)
    c = lax.rem(s, 2)
    s1 = (s1a, s1b)
    started = []

    def place(px, pz, pc):
        return (px * 4 + pz) * 2 + pc

    def ring(axis, k):
        if axis == "y":
            return (s, wrap(y + k))
        if axis == "x":
            return (place(wrap(x + k), z, c), y)
        return (place(x, wrap(z + k), c), y)

    sibling = (place(x, z, 1 - c), y)
    peers = [ring("y", 1), ring("y", -1), sibling]
    peers += [ring(a, k) for a in ("x", "z") for k in (1, 2, 3)]

    def remote(src, dst, send, recv, device):
        copy = pltpu.make_async_remote_copy(
            src_ref=src, dst_ref=dst, send_sem=send, recv_sem=recv,
            device_id=device, device_id_type=MESH,
        )
        copy.start()
        started.append(copy)
        return copy

    tok_local = pltpu.make_async_copy(tok, tk.at[0], loc_sem.at[0])
    tok_local.start()
    w_local = []
    for d in (0, 3, 1, 2):
        rows = pl.ds(pl.multiple_of(wrap(y + d) * FEAT, FEAT), FEAT)
        for j, ref in enumerate((wq, wk, wv)):
            copy = pltpu.make_async_copy(ref.at[rows, :], w.at[d, j], wloc_sem.at[d, j])
            copy.start()
            w_local.append(copy)
    mine = pl.ds(pl.multiple_of(y * FEAT, FEAT), FEAT)
    wo_local = pltpu.make_async_copy(wo.at[:, mine], wov.at[0], loc_sem.at[1])
    wo_local.start()

    barrier = pltpu.get_barrier_semaphore()
    for peer in peers:
        pl.semaphore_signal(barrier, inc=1, device_id=peer, device_id_type=MESH)
    pl.semaphore_wait(barrier, len(peers))

    tok_c = {}
    for i in range(NB):
        rows = pl.ds(i * BLK, BLK)
        tok_c[i, 0] = remote(tok.at[rows, :], tk.at[3, rows, :], tok_s.at[i, 0], tok_r.at[i, 0], ring("y", 1))
        tok_c[i, 1] = remote(tok.at[rows, :], tk.at[1, rows, :], tok_s.at[i, 1], tok_r.at[i, 1], ring("y", -1))

    lane = lax.broadcasted_iota(jnp.int32, (8, 128), 1)
    row = jnp.zeros((8, 128), jnp.int32)
    for i in range(NB):
        row = jnp.where(lane == s * NB + i, ids[i], row)

    def spread(stage, row, targets):
        idsend[stage] = row
        copies = []
        for k, target in targets:
            copies.append(
                remote(idsend.at[stage], idg.at[stage, k - 1], id_s.at[stage, k - 1], id_r.at[stage, k - 1], target)
            )
        return copies

    ids_x = spread(0, row, [(k, ring("x", k)) for k in (1, 2, 3)])

    tok_local.wait()
    for copy in w_local[:3]:
        copy.wait()

    def own_tile(t, carry):
        n, m = t // 2, lax.rem(t, 2)
        rows = pl.ds(pl.multiple_of(m * 256, 256), 256)
        cols = pl.ds(pl.multiple_of(lax.rem(n, 2) * 256, 256), 256)
        acc[n, rows, :] = jnp.dot(tk[0, rows, :], w[0, n // 2, :, cols], preferred_element_type=F32)
        return carry

    lax.fori_loop(0, 12, own_tile, 0)

    for copy in ids_x:
        copy.wait_recv()
    row = row + idg[0, 0] + idg[0, 1] + idg[0, 2]
    ids_z = spread(1, row, [(k, ring("z", k)) for k in (1, 2, 3)])
    for copy in w_local[3:]:
        copy.wait()

    tok_f = {}
    ag = {}
    axes = ("x", "z")

    def forward_tokens(i):
        lo, hi = pl.ds(i * BLK, HALF), pl.ds(i * BLK + HALF, HALF)
        tok_c[i, 0].wait_recv()
        tok_f[i, 0] = remote(tk.at[3, lo, :], tk.at[2, lo, :], tok_s.at[i, 2], tok_r.at[i, 2], ring("y", 1))
        tok_c[i, 1].wait_recv()
        tok_f[i, 1] = remote(tk.at[1, hi, :], tk.at[2, hi, :], tok_s.at[i, 3], tok_r.at[i, 3], ring("y", -1))

    def near_tiles(i):
        rows = pl.ds(i * BLK, BLK)

        def tile(n, carry):
            cols = pl.ds(pl.multiple_of(lax.rem(n, 2) * 256, 256), 256)
            acc[n, rows, :] += jnp.dot(
                tk[3, rows, :], w[3, n // 2, :, cols], preferred_element_type=F32
            ) + jnp.dot(tk[1, rows, :], w[1, n // 2, :, cols], preferred_element_type=F32)
            return carry

        lax.fori_loop(0, 6, tile, 0)

    def far_tiles(i):
        rows = pl.ds(i * BLK, BLK)
        tok_f[i, 0].wait_recv()
        tok_f[i, 1].wait_recv()

        def tile(n, carry):
            cols = pl.ds(pl.multiple_of(lax.rem(n, 2) * 256, 256), 256)
            acc[n, rows, :] += jnp.dot(tk[2, rows, :], w[2, n // 2, :, cols], preferred_element_type=F32)
            return carry

        lax.fori_loop(0, 6, tile, 0)
        for f in range(2):
            qs[f, i] = acc[f, rows, :].astype(BF16)
            s1[f][0, 0, i, :, :256] = acc[2 + f, rows, :].astype(BF16)
            s1[f][0, 0, i, :, 256:] = acc[4 + f, rows, :].astype(BF16)

    def gather_send(i):
        for f in range(2):
            own, a = s1[f].at[0, 0, i], axes[f]
            ag[f, i, 0] = remote(own, s1[f].at[0, 3, i], ag_s.at[f, i, 0], ag_r.at[f, i, 0], ring(a, 1))
            ag[f, i, 1] = remote(own, s1[f].at[0, 1, i], ag_s.at[f, i, 1], ag_r.at[f, i, 1], ring(a, -1))
            ag[f, i, 2] = remote(own, s1[f].at[1, 0, i], ag_s.at[f, i, 2], ag_r.at[f, i, 2], sibling)

    def gather_forward(i):
        lo, hi = pl.ds(0, HALF), pl.ds(HALF, HALF)
        for f in range(2):
            g, a = s1[f], axes[f]
            ag[f, i, 0].wait_recv()
            ag[f, i, 3] = remote(g.at[0, 3, i, lo], g.at[0, 2, i, lo], ag_s.at[f, i, 3], ag_r.at[f, i, 3], ring(a, 1))
            ag[f, i, 5] = remote(g.at[0, 3, i], g.at[1, 3, i], ag_s.at[f, i, 5], ag_r.at[f, i, 5], sibling)
            ag[f, i, 1].wait_recv()
            ag[f, i, 4] = remote(g.at[0, 1, i, hi], g.at[0, 2, i, hi], ag_s.at[f, i, 4], ag_r.at[f, i, 4], ring(a, -1))
            ag[f, i, 6] = remote(g.at[0, 1, i], g.at[1, 1, i], ag_s.at[f, i, 6], ag_r.at[f, i, 6], sibling)

    def gather_far(i):
        for f in range(2):
            g = s1[f]
            ag[f, i, 3].wait_recv()
            ag[f, i, 4].wait_recv()
            ag[f, i, 7] = remote(g.at[0, 2, i], g.at[1, 2, i], ag_s.at[f, i, 7], ag_r.at[f, i, 7], sibling)

    forward_tokens(0)
    near_tiles(0)
    for copy in ids_z:
        copy.wait_recv()
    row = row + idg[1, 0] + idg[1, 1] + idg[1, 2]
    ids_c = spread(2, row, [(1, sibling)])
    forward_tokens(1)
    near_tiles(1)
    far_tiles(0)
    gather_send(0)
    ids_c[0].wait_recv()
    row = row + idg[2, 0]

    across = jnp.broadcast_to(row[0:1, :], (128, 128))
    down = across.T
    one = lax.broadcasted_iota(jnp.int32, (128, 128), 0)
    two = lax.broadcasted_iota(jnp.int32, (128, 128), 1)
    same = (across == down) & (one != two)
    partner = jnp.sum(jnp.where(same, one + 1, 0), axis=0, keepdims=True) - 1
    part_v[...] = jnp.broadcast_to(partner, (8, 128))
    part_copy = pltpu.make_async_copy(part_v, part_s, loc_sem.at[2])
    part_copy.start()

    forward_tokens(2)
    near_tiles(2)
    far_tiles(1)
    gather_send(1)
    gather_forward(0)
    forward_tokens(3)
    near_tiles(3)

    lo = pl.ds(pl.multiple_of(c * 256, 256), 128)
    hi = pl.ds(pl.multiple_of(c * 256 + 128, 128), 128)
    both = pl.ds(pl.multiple_of(c * 256, 256), 256)

    def columns(k):
        return pl.ds(pl.multiple_of(wrap(y + k) * FEAT, FEAT), FEAT)

    wo_c = [
        remote(wo.at[lo, columns(2)], wrel.at[0], wo_s.at[0], wo_r.at[0], ring("y", 1)),
        remote(wo.at[hi, columns(2)], wrel.at[1], wo_s.at[1], wo_r.at[1], ring("y", -1)),
        remote(wo.at[both, columns(1)], wov.at[3, both], wo_s.at[2], wo_r.at[2], ring("y", 1)),
        remote(wo.at[both, columns(-1)], wov.at[1, both], wo_s.at[3], wo_r.at[3], ring("y", -1)),
    ]
    far_tiles(2)
    gather_send(2)
    gather_forward(1)
    gather_far(0)
    far_tiles(3)
    gather_send(3)
    gather_forward(2)
    gather_far(1)
    gather_forward(3)
    gather_far(2)
    wo_c[0].wait_recv()
    wo_f0 = remote(wrel.at[0], wov.at[2, lo], wo_s.at[4], wo_r.at[4], ring("y", 1))
    wo_c[1].wait_recv()
    wo_f1 = remote(wrel.at[1], wov.at[2, hi], wo_s.at[5], wo_r.at[5], ring("y", -1))
    gather_far(3)
    part_copy.wait()

    def choice(f, k, i):
        dest = place(x, wrap(z + k), c) if f == 0 else place(wrap(x + k), z, c)
        p = part_s[0, dest * NB + i]
        at = jnp.maximum(p, 0)
        xp, zp = at // 32, lax.rem(at // 8, 4)
        cp, ip = lax.rem(at // 4, 2), lax.rem(at, 4)
        along, held = (xp - x, zp) if f == 0 else (zp - z, xp)
        return (lax.rem(cp + c, 2), wrap(along), ip), held, p

    second = ("z", "x")
    here = (z, x)
    for f in range(2):
        for i in range(NB):
            for k in (2, 5, 6, 7):
                ag[f, i, k].wait_recv()

    def fill(f, g, k, slots, relay=None):
        for n, i in enumerate(slots):
            index, held, _ = choice(f, k, i)
            packet = s1[f][index[0], index[1], index[2]]
            if relay is not None:
                packet = jnp.where(held == here[f], packet, rel[f, relay, n])
            tx[f, g, n] = packet

    rs = {}
    for f in range(2):
        right, left = ring(second[f], 1), ring(second[f], -1)
        fill(f, 0, 2, (0, 1))
        rs[f, 0] = remote(tx.at[f, 0], rel.at[f, 0], rs_s.at[f, 0], rs_r.at[f, 0], right)
        fill(f, 1, 2, (2, 3))
        rs[f, 1] = remote(tx.at[f, 1], rel.at[f, 1], rs_s.at[f, 1], rs_r.at[f, 1], left)
    for f in range(2):
        right, left = ring(second[f], 1), ring(second[f], -1)
        fill(f, 2, 1, (2, 3))
        rs[f, 2] = remote(tx.at[f, 2], fin.at[f, 0, pl.ds(2, 2)], rs_s.at[f, 2], rs_r.at[f, 2], right)
        fill(f, 3, -1, (0, 1))
        rs[f, 3] = remote(tx.at[f, 3], fin.at[f, 1, pl.ds(0, 2)], rs_s.at[f, 3], rs_r.at[f, 3], left)
    for f in range(2):
        right, left = ring(second[f], 1), ring(second[f], -1)
        rs[f, 0].wait_recv()
        fill(f, 4, 1, (0, 1), 0)
        rs[f, 4] = remote(tx.at[f, 4], fin.at[f, 0, pl.ds(0, 2)], rs_s.at[f, 4], rs_r.at[f, 4], right)
        rs[f, 1].wait_recv()
        fill(f, 5, -1, (2, 3), 1)
        rs[f, 5] = remote(tx.at[f, 5], fin.at[f, 1, pl.ds(2, 2)], rs_s.at[f, 5], rs_r.at[f, 5], left)

    wo_x = []
    for n, (d, ready) in enumerate(((3, wo_c[2:3]), (1, wo_c[3:4]), (2, [wo_f0, wo_f1]))):
        for copy in ready:
            copy.wait_recv()
        wo_x.append(remote(wov.at[d, both], wov.at[d, both], wo_s.at[6 + n], wo_r.at[6 + n], sibling))

    def attend(i):
        rows = pl.ds(i * BLK, BLK)
        for f in range(2):
            index, held, p = choice(f, 0, i)
            from_left = (held == wrap(here[f] - 1)) | ((held == wrap(here[f] + 2)) & (i < 2))
            packet = jnp.where(from_left, fin[f, 0, i], fin[f, 1, i])
            kvp[f] = jnp.where(held == here[f], s1[f][index[0], index[1], index[2]], packet)
            for j in range(2):
                kc, vc = pl.ds(j * HDIM, HDIM), pl.ds(256 + j * HDIM, HDIM)
                query = qs[f, i, :, kc]
                dims = (((1,), (1,)), ((), ()))
                near = lax.dot_general(query, s1[f][0, 0, i, :, kc], dims, preferred_element_type=F32) * SCALE
                far = lax.dot_general(query, kvp[f, :, kc], dims, preferred_element_type=F32) * SCALE
                far = jnp.where(p >= 0, far, -1e30)
                top = jnp.maximum(jnp.max(near, axis=1, keepdims=True), jnp.max(far, axis=1, keepdims=True))
                near, far = jnp.exp(near - top), jnp.exp(far - top)
                total = jnp.sum(near, axis=1, keepdims=True) + jnp.sum(far, axis=1, keepdims=True)
                near, far = (near / total).astype(BF16), (far / total).astype(BF16)
                mixed = jnp.dot(near, s1[f][0, 0, i, :, vc], preferred_element_type=F32)
                mixed += jnp.dot(far, kvp[f, :, vc], preferred_element_type=F32)
                mx[0, rows, pl.ds((2 * f + j) * HDIM, HDIM)] = mixed.astype(BF16)

    for f in range(2):
        for g in (2, 3, 4, 5):
            rs[f, g].wait_recv()

    mx_c = {}

    def send_mixed(i):
        rows = pl.ds(i * BLK, BLK)
        mx_c[i, 0] = remote(mx.at[0, rows], mx.at[3, rows], mx_s.at[i, 0], mx_r.at[i, 0], ring("y", 1))
        mx_c[i, 1] = remote(mx.at[0, rows], mx.at[1, rows], mx_s.at[i, 1], mx_r.at[i, 1], ring("y", -1))

    def forward_mixed(i):
        lo, hi = pl.ds(i * BLK, HALF), pl.ds(i * BLK + HALF, HALF)
        mx_c[i, 0].wait_recv()
        mx_c[i, 2] = remote(mx.at[3, lo], mx.at[2, lo], mx_s.at[i, 2], mx_r.at[i, 2], ring("y", 1))
        mx_c[i, 1].wait_recv()
        mx_c[i, 3] = remote(mx.at[1, hi], mx.at[2, hi], mx_s.at[i, 3], mx_r.at[i, 3], ring("y", -1))

    def project(i):
        rows = pl.ds(i * BLK, BLK)
        mx_c[i, 2].wait_recv()
        mx_c[i, 3].wait_recv()

        def tile(n, carry):
            cols = pl.ds(pl.multiple_of(n * 256, 256), 256)
            total = jnp.dot(mx[0, rows, :], wov[0, :, cols], preferred_element_type=F32)
            for d in (1, 2, 3):
                total += jnp.dot(mx[d, rows, :], wov[d, :, cols], preferred_element_type=F32)
            out[rows, cols] = total.astype(BF16)
            return carry

        lax.fori_loop(0, 4, tile, 0)

    for i in range(NB):
        attend(i)
        send_mixed(i)
        if i:
            forward_mixed(i - 1)
    forward_mixed(NB - 1)
    wo_local.wait()
    for copy in wo_x:
        copy.wait_recv()
    for i in range(NB):
        project(i)
    for copy in started:
        copy.wait_send()


def per_device(tokens, w_query, w_key, w_value, w_out, block_bucket):
    anywhere = pl.BlockSpec(memory_space=pl.ANY)
    dma = pltpu.SemaphoreType.DMA
    return pl.pallas_call(
        kernel,
        out_shape=jax.ShapeDtypeStruct((NB * BLK, FEAT), BF16),
        in_specs=[pl.BlockSpec(memory_space=pltpu.SMEM)] + [anywhere] * 5,
        out_specs=pl.BlockSpec(memory_space=pltpu.VMEM),
        scratch_shapes=[
            pltpu.VMEM((4, NB * BLK, FEAT), BF16),
            pltpu.VMEM((4, 3, FEAT, WIDTH), BF16),
            pltpu.VMEM((6, NB * BLK, 256), F32),
            pltpu.VMEM((2, NB, BLK, 256), BF16),
            pltpu.VMEM((2, 4, NB, BLK, PACK), BF16),
            pltpu.VMEM((2, 4, NB, BLK, PACK), BF16),
            pltpu.VMEM((2, 6, 2, BLK, PACK), BF16),
            pltpu.VMEM((2, 2, 2, BLK, PACK), BF16),
            pltpu.VMEM((2, 2, NB, BLK, PACK), BF16),
            pltpu.VMEM((2, BLK, PACK), BF16),
            pltpu.VMEM((4, WIDTH, FEAT), BF16),
            pltpu.VMEM((2, 128, FEAT), BF16),
            pltpu.VMEM((4, NB * BLK, WIDTH), BF16),
            pltpu.VMEM((3, 3, 8, 128), jnp.int32),
            pltpu.VMEM((3, 8, 128), jnp.int32),
            pltpu.VMEM((8, 128), jnp.int32),
            pltpu.SMEM((8, 128), jnp.int32),
            dma((3,)),
            dma((4, 3)),
            dma((NB, 4)),
            dma((NB, 4)),
            dma((3, 3)),
            dma((3, 3)),
            dma((2, NB, 8)),
            dma((2, NB, 8)),
            dma((2, 6)),
            dma((2, 6)),
            dma((9,)),
            dma((9,)),
            dma((NB, 4)),
            dma((NB, 4)),
        ],
        compiler_params=pltpu.CompilerParams(
            collective_id=0, has_side_effects=True, vmem_limit_bytes=58 * 2**20
        ),
    )(block_bucket, tokens, w_query, w_key, w_value, w_out)


def solution(mesh):
    placed = (
        P("seq", "head"),
        P(None, "head"),
        P(None, "head"),
        P(None, "head"),
        P("head", None),
        P("seq"),
    )
    return jax.shard_map(
        per_device, mesh=mesh, in_specs=placed, out_specs=P("seq", "head"), check_vma=False
    )
```

time: 515 us -> 109 us (0.21)
  waiting for transfers between devices: 221 us -> 0 us
  Pallas kernels: 0 us -> 107 us
  blocking collectives: 80.9 us -> 0 us
  other arithmetic: 65.6 us -> 0 us
  local copies, waits for them, and re-layouts: 65.2 us -> 2.26 us
  starting transfers between devices: 32.9 us -> 0 us
  matrix products: 31.7 us -> 0 us
  between operations: 13.6 us -> 0.01 us
    all_to_all x4 -> x0, waiting for transfers between devices: 182 us -> none  [the longest x2 76 us: exchange_in_pieces(): lax.all_to_all(share, axis, split_axis=0, concat_axis=0, tiled=True)]
    pallas_call x0 -> x1, Pallas kernels: none -> 107 us  [per_device(): pl.pallas_call(kernel, out_shape=jax.ShapeDtypeStruct((NB * BLK, FEAT), B...]
    all_to_all x1 -> x0, blocking collectives: 80.9 us -> none  [exchange_in_pieces(): lax.all_to_all(share, axis, split_axis=0, concat_axis=0, tiled=True)]
    all_gather x2 -> x0, waiting for transfers between devices: 37.4 us -> none  [the longest x1 37.4 us: per_device(): piece = lax.all_gather(tokens, 'head', axis=1, tiled=True)]
    all_to_all x4 -> x0, starting transfers between devices: 32.9 us -> none  [the longest x2 14.3 us: exchange_in_pieces(): lax.all_to_all(share, axis, split_axis=0, concat_axis=0, tiled=True)]
    dot_general x12 -> x0, matrix products: 31.7 us -> none  [the longest x3 10.7 us: per_device(): jnp.dot(piece, weight, preferred_element_type=jnp.float32)]
    gather x12 -> x0, local copies, waits for them, and re-layouts: 28.1 us -> none  [the longest x4 8.62 us: head_attend(): jnp.take(value_head, index, axis=0)]
    select_n x14 -> x0, other arithmetic: 26.7 us -> none  [the longest x8 16 us: head_attend(): jnp.take(key_head, index, axis=0)]
  transfers between devices with their start and end apart: 6 -> 0, of which waited for: 4 -> 0; matrix products, arithmetic and copies ran while one was open for 11% -> 0% of each run, Pallas kernels for 0% -> 0%
where the time goes in v1:
time: 109 us
  Pallas kernels  107 us (98%)
  local copies, waits for them, and re-layouts  2.26 us (2%)
    pallas_call x1, Pallas kernels, per_device(): pl.pallas_call(kernel, out_shape=jax.ShapeDtypeStruct((NB * BLK, FEAT), B...  107 us
    unnamed x1, local copies, waits for them, and re-layouts  2.26 us

profile of v1, /device:TPU:1, one launch (start us, length us, event | category | flops | bytes accessed | tf_op | source)
XLA Modules:
  0.0 109.2 jit_solution(18380578729813077582)
XLA Ops:
  0.0 106.9 %shard_map.64 = bf16[512,1024]{1,0:T(8,128)(2,1)} custom-call(s32[4]{0:T(128)} %ids.1, bf16[512,1024]{1,0:T(8,128)(2,1)} %tok.1, bf16[4096,512]{1,0:T(8,128)(2,1)} %wq.1, bf16[4096,512]{1,0:T(8,128)(2,1)} %wk.1, bf16[4096,512]{1,0:T(8,128)(2,1)} %wv.1, bf16[512,4096]{1,0:T(8,128)(2,1)} %wo.1), custom_call_target="tpu_custom_call" | custom-call | tf_op jit(solution)/shard_map/pallas_call | solution.py:372
  106.9 2.3 %copy.8 = bf16[512,1024]{1,0:T(8,128)(2,1)} copy(bf16[512,1024]{1,0:T(8,128)(2,1)} %shard_map.64) | data formatting | bytes 2097152

commit v2 on v1

v2 whole, which is shorter than its diff:
```python
import jax
import jax.numpy as jnp
from jax import lax
from jax.experimental import pallas as pl
from jax.experimental.pallas import tpu as pltpu
from jax.sharding import PartitionSpec as P

HDIM = 128
SCALE = HDIM ** (-0.5)
BLK = 128
HALF = BLK // 2
NB = 4
FEAT = 1024
WIDTH = 512
PACK = 512
MESH = pl.DeviceIdType.MESH
F32 = jnp.float32
BF16 = jnp.bfloat16


def wrap(n):
    return lax.rem(n + 4, 4)


def kernel(
    ids, tok, wq, wk, wv, wo, out,
    tk, w, acc, qs, s1a, s1b, tx, rel, fin, kvp, wov, mx,
    idg, idsend, part_v, part_s,
    loc_sem, wloc_sem, tok_s, tok_r, id_s, id_r, ag_s, ag_r, rs_s, rs_r, wo_s, wo_r, mx_s, mx_r,
):
    s = lax.axis_index("seq")
    y = lax.axis_index("head")
    x = s // 8
    z = lax.rem(s // 2, 4)
    c = lax.rem(s, 2)
    s1 = (s1a, s1b)
    wo6 = wo.reshape(4, 4, 2, 16, 4 * FEAT)
    started = []

    def place(px, pz, pc):
        return (px * 4 + pz) * 2 + pc

    def ring(axis, k):
        if axis == "y":
            return (s, wrap(y + k))
        if axis == "x":
            return (place(wrap(x + k), z, c), y)
        return (place(x, wrap(z + k), c), y)

    sibling = (place(x, z, 1 - c), y)
    peers = [sibling] + [ring(a, k) for a in ("y", "x", "z") for k in (1, 2, 3)]

    def remote(src, dst, send, recv, device):
        copy = pltpu.make_async_remote_copy(
            src_ref=src, dst_ref=dst, send_sem=send, recv_sem=recv,
            device_id=device, device_id_type=MESH,
        )
        copy.start()
        started.append(copy)
        return copy

    tok_local = pltpu.make_async_copy(tok, tk.at[0], loc_sem.at[0])
    tok_local.start()
    w_local = []
    for d in (0, 3, 1, 2):
        rows = pl.ds(pl.multiple_of(wrap(y + d) * FEAT, FEAT), FEAT)
        for j, ref in enumerate((wq, wk, wv)):
            copy = pltpu.make_async_copy(ref.at[rows, :], w.at[d, j], wloc_sem.at[d, j])
            copy.start()
            w_local.append(copy)
    mine = pl.ds(pl.multiple_of(y * FEAT, FEAT), FEAT)
    wo_local = pltpu.make_async_copy(wo6.at[:, :, :, :, mine], wov.at[0], loc_sem.at[1])
    wo_local.start()

    barrier = pltpu.get_barrier_semaphore()
    for peer in peers:
        pl.semaphore_signal(barrier, inc=1, device_id=peer, device_id_type=MESH)
    pl.semaphore_wait(barrier, len(peers))

    wo_y = []
    row16 = pl.ds(pl.multiple_of(s * 16, 16), 16)
    for k in (1, 2, 3):
        cols = pl.ds(pl.multiple_of(wrap(y + k) * FEAT, FEAT), FEAT)
        wo_y.append(remote(wo.at[row16, cols], wov.at[4 - k, x, z, c], wo_s.at[k - 1], wo_r.at[k - 1], ring("y", k)))

    tok_c = {}
    tok_f = {}

    def send_tokens(k):
        rows = pl.ds(k * HALF, HALF)
        tok_c[k, 0] = remote(tok.at[rows, :], tk.at[3, rows, :], tok_s.at[k, 0], tok_r.at[k, 0], ring("y", 1))
        tok_c[k, 1] = remote(tok.at[rows, :], tk.at[1, rows, :], tok_s.at[k, 1], tok_r.at[k, 1], ring("y", -1))

    def tokens_event(k):
        lo, hi = pl.ds(k * HALF, HALF // 2), pl.ds(k * HALF + HALF // 2, HALF // 2)
        tok_c[k, 0].wait_recv()
        tok_f[k, 0] = remote(tk.at[3, lo, :], tk.at[2, lo, :], tok_s.at[k, 2], tok_r.at[k, 2], ring("y", 1))
        tok_c[k, 1].wait_recv()
        tok_f[k, 1] = remote(tk.at[1, hi, :], tk.at[2, hi, :], tok_s.at[k, 3], tok_r.at[k, 3], ring("y", -1))
        if k + 2 < 8:
            send_tokens(k + 2)

    send_tokens(0)
    send_tokens(1)

    lane = lax.broadcasted_iota(jnp.int32, (8, 128), 1)
    row = jnp.zeros((8, 128), jnp.int32)
    for i in range(NB):
        row = jnp.where(lane == s * NB + i, ids[i], row)

    def spread(stage, row, targets):
        idsend[stage] = row
        copies = []
        for k, target in targets:
            copies.append(
                remote(idsend.at[stage], idg.at[stage, k - 1], id_s.at[stage, k - 1], id_r.at[stage, k - 1], target)
            )
        return copies

    ids_x = spread(0, row, [(k, ring("x", k)) for k in (1, 2, 3)])

    tok_local.wait()
    for copy in w_local[:3]:
        copy.wait()

    def own_tile(t, carry):
        n, m = t // 2, lax.rem(t, 2)
        rows = pl.ds(pl.multiple_of(m * 256, 256), 256)
        cols = pl.ds(pl.multiple_of(lax.rem(n, 2) * 256, 256), 256)
        acc[n, rows, :] = jnp.dot(tk[0, rows, :], w[0, n // 2, :, cols], preferred_element_type=F32)
        return carry

    lax.fori_loop(0, 12, own_tile, 0)

    def near_tiles(i):
        rows = pl.ds(i * BLK, BLK)

        def tile(n, carry):
            cols = pl.ds(pl.multiple_of(lax.rem(n, 2) * 256, 256), 256)
            acc[n, rows, :] += jnp.dot(
                tk[3, rows, :], w[3, n // 2, :, cols], preferred_element_type=F32
            ) + jnp.dot(tk[1, rows, :], w[1, n // 2, :, cols], preferred_element_type=F32)
            return carry

        lax.fori_loop(0, 6, tile, 0)

    def far_tiles(i, first, last):
        rows = pl.ds(i * BLK, BLK)

        def tile(n, carry):
            cols = pl.ds(pl.multiple_of(lax.rem(n, 2) * 256, 256), 256)
            acc[n, rows, :] += jnp.dot(tk[2, rows, :], w[2, n // 2, :, cols], preferred_element_type=F32)
            return carry

        lax.fori_loop(first, last, tile, 0)

    ag = {}
    axes = ("x", "z")

    def finish_keys(i):
        rows = pl.ds(i * BLK, BLK)
        for k in (2 * i, 2 * i + 1):
            tok_f[k, 0].wait_recv()
            tok_f[k, 1].wait_recv()
        far_tiles(i, 2, 6)
        for f in range(2):
            s1[f][0, 0, i, :, :256] = acc[2 + f, rows, :].astype(BF16)
            s1[f][0, 0, i, :, 256:] = acc[4 + f, rows, :].astype(BF16)
        for f in range(2):
            own, a = s1[f].at[0, 0, i], axes[f]
            for n, (k, d) in enumerate(((2, 2), (1, 3), (-1, 1))):
                ag[f, i, d] = remote(own, s1[f].at[0, d, i], ag_s.at[f, i, n], ag_r.at[f, i, n], ring(a, k))
            ag[f, i, "own"] = remote(own, s1[f].at[1, 0, i], ag_s.at[f, i, 3], ag_r.at[f, i, 3], sibling)

    def finish_query(i):
        rows = pl.ds(i * BLK, BLK)
        far_tiles(i, 0, 2)
        for f in range(2):
            qs[f, i] = acc[f, rows, :].astype(BF16)

    def to_sibling(i):
        for n, d in ((0, 3), (1, 1), (2, 2)):
            for f in range(2):
                ag[f, i, d].wait_recv()
                ag[f, i, "s", d] = remote(
                    s1[f].at[0, d, i], s1[f].at[1, d, i], ag_s.at[f, i, 4 + n], ag_r.at[f, i, 4 + n], sibling
                )

    for copy in ids_x:
        copy.wait_recv()
    row = row + idg[0, 0] + idg[0, 1] + idg[0, 2]
    ids_z = spread(1, row, [(k, ring("z", k)) for k in (1, 2, 3)])

    for copy in wo_y:
        copy.wait_recv()
    left_cols, right_cols = pl.ds(0, 512), pl.ds(512, 512)
    three = pl.ds(1, 3)
    wo_1 = []
    for k in (2, 1, 3):
        own = wov.at[three, x, z, c, :, left_cols]
        wo_1.append(remote(own, own, wo_s.at[2 + k], wo_r.at[2 + k], ring("x", k)))
        own = wov.at[three, x, z, c, :, right_cols]
        wo_1.append(remote(own, own, wo_s.at[5 + k], wo_r.at[5 + k], ring("z", k)))

    tokens_event(0)
    for copy in w_local[3:]:
        copy.wait()
    for copy in ids_z:
        copy.wait_recv()
    row = row + idg[1, 0] + idg[1, 1] + idg[1, 2]
    ids_c = spread(2, row, [(1, sibling)])
    tokens_event(1)

    for copy in wo_1:
        copy.wait_recv()
    wo_2 = []
    for k in (2, 1, 3):
        own = wov.at[three, :, z, c, :, left_cols]
        wo_2.append(remote(own, own, wo_s.at[8 + k], wo_r.at[8 + k], ring("z", k)))
        own = wov.at[three, x, :, c, :, right_cols]
        wo_2.append(remote(own, own, wo_s.at[11 + k], wo_r.at[11 + k], ring("x", k)))

    near_tiles(0)
    ids_c[0].wait_recv()
    row = row + idg[2, 0]

    across = jnp.broadcast_to(row[0:1, :], (128, 128))
    down = across.T
    one = lax.broadcasted_iota(jnp.int32, (128, 128), 0)
    two = lax.broadcasted_iota(jnp.int32, (128, 128), 1)
    same = (across == down) & (one != two)
    partner = jnp.sum(jnp.where(same, one + 1, 0), axis=0, keepdims=True) - 1
    part_v[...] = jnp.broadcast_to(partner, (8, 128))
    part_copy = pltpu.make_async_copy(part_v, part_s, loc_sem.at[2])
    part_copy.start()

    tokens_event(2)
    finish_keys(0)
    tokens_event(3)
    finish_query(0)
    near_tiles(1)
    tokens_event(4)
    finish_keys(1)
    for copy in wo_2:
        copy.wait_recv()
    own = wov.at[three, :, :, c]
    wo_3 = remote(own, own, wo_s.at[15], wo_r.at[15], sibling)
    tokens_event(5)
    near_tiles(2)
    to_sibling(0)
    tokens_event(6)
    finish_query(1)
    finish_keys(2)
    tokens_event(7)
    near_tiles(3)
    to_sibling(1)
    finish_keys(3)
    finish_query(2)
    to_sibling(2)
    finish_query(3)
    part_copy.wait()
    to_sibling(3)

    def choice(f, k, i):
        dest = place(x, wrap(z + k), c) if f == 0 else place(wrap(x + k), z, c)
        p = part_s[0, dest * NB + i]
        at = jnp.maximum(p, 0)
        xp, zp = at // 32, lax.rem(at // 8, 4)
        cp, ip = lax.rem(at // 4, 2), lax.rem(at, 4)
        along, held = (xp - x, zp) if f == 0 else (zp - z, xp)
        return (lax.rem(cp + c, 2), wrap(along), ip), held, p

    second = ("z", "x")
    here = (z, x)
    for f in range(2):
        for i in range(NB):
            ag[f, i, "own"].wait_recv()
            for d in (1, 2, 3):
                ag[f, i, "s", d].wait_recv()

    low, high = pl.ds(0, HALF), pl.ds(HALF, HALF)
    rs = {}

    def pass_on(f, i, g, k, rows, to, dst, relay=None):
        index, held, _ = choice(f, k, i)
        packet = s1[f][index[0], index[1], index[2], rows]
        if relay is not None:
            packet = jnp.where(held == here[f], packet, rel[f, i, relay])
        tx[f, i, g] = packet
        rs[f, i, g] = remote(tx.at[f, i, g], dst, rs_s.at[f, i, g], rs_r.at[f, i, g], ring(second[f], to))

    def relay_out(i):
        for f in range(2):
            pass_on(f, i, 0, 2, low, 1, rel.at[f, i, 0])
            pass_on(f, i, 1, 2, high, -1, rel.at[f, i, 1])

    def direct_out(i):
        for f in range(2):
            pass_on(f, i, 2, 1, high, 1, fin.at[f, 0, i, high])
            pass_on(f, i, 3, -1, low, -1, fin.at[f, 1, i, low])

    def merged_out(i):
        for f in range(2):
            rs[f, i, 0].wait_recv()
            pass_on(f, i, 4, 1, low, 1, fin.at[f, 0, i, low], 0)
            rs[f, i, 1].wait_recv()
            pass_on(f, i, 5, -1, high, -1, fin.at[f, 1, i, high], 1)

    def attend(i):
        rows = pl.ds(i * BLK, BLK)
        for f in range(2):
            for g in (2, 3, 4, 5):
                rs[f, i, g].wait_recv()
        for f in range(2):
            index, held, p = choice(f, 0, i)
            at_left, at_right = held == wrap(here[f] - 1), held == wrap(here[f] + 1)
            for half, from_left in ((low, jnp.logical_not(at_right)), (high, at_left)):
                packet = jnp.where(from_left, fin[f, 0, i, half], fin[f, 1, i, half])
                own = s1[f][index[0], index[1], index[2], half]
                kvp[f, half] = jnp.where(held == here[f], own, packet)
            for j in range(2):
                kc, vc = pl.ds(j * HDIM, HDIM), pl.ds(256 + j * HDIM, HDIM)
                query = qs[f, i, :, kc]
                dims = (((1,), (1,)), ((), ()))
                near = lax.dot_general(query, s1[f][0, 0, i, :, kc], dims, preferred_element_type=F32) * SCALE
                far = lax.dot_general(query, kvp[f, :, kc], dims, preferred_element_type=F32) * SCALE
                far = jnp.where(p >= 0, far, -1e30)
                top = jnp.maximum(jnp.max(near, axis=1, keepdims=True), jnp.max(far, axis=1, keepdims=True))
                near, far = jnp.exp(near - top), jnp.exp(far - top)
                total = jnp.sum(near, axis=1, keepdims=True) + jnp.sum(far, axis=1, keepdims=True)
                near, far = (near / total).astype(BF16), (far / total).astype(BF16)
                mixed = jnp.dot(near, s1[f][0, 0, i, :, vc], preferred_element_type=F32)
                mixed += jnp.dot(far, kvp[f, :, vc], preferred_element_type=F32)
                mx[0, rows, pl.ds((2 * f + j) * HDIM, HDIM)] = mixed.astype(BF16)

    mx_c = {}

    def send_mixed(i):
        rows = pl.ds(i * BLK, BLK)
        if i == NB - 1:
            mx_c[i, 2] = remote(mx.at[0, rows], mx.at[2, rows], mx_s.at[i, 2], mx_r.at[i, 2], ring("y", 2))
        mx_c[i, 0] = remote(mx.at[0, rows], mx.at[3, rows], mx_s.at[i, 0], mx_r.at[i, 0], ring("y", 1))
        mx_c[i, 1] = remote(mx.at[0, rows], mx.at[1, rows], mx_s.at[i, 1], mx_r.at[i, 1], ring("y", -1))

    def forward_mixed(i):
        lo, hi = pl.ds(i * BLK, HALF), pl.ds(i * BLK + HALF, HALF)
        mx_c[i, 0].wait_recv()
        mx_c[i, 2] = remote(mx.at[3, lo], mx.at[2, lo], mx_s.at[i, 2], mx_r.at[i, 2], ring("y", 1))
        mx_c[i, 1].wait_recv()
        mx_c[i, 3] = remote(mx.at[1, hi], mx.at[2, hi], mx_s.at[i, 3], mx_r.at[i, 3], ring("y", -1))

    def project(i):
        rows = pl.ds(i * BLK, BLK)
        for n in (0, 1, 2) if i == NB - 1 else (2, 3):
            mx_c[i, n].wait_recv()

        def tile(n, carry):
            cols = pl.ds(pl.multiple_of(n * 256, 256), 256)
            total = jnp.dot(mx[0, rows, :], wov[0, :, :, :, :, cols].reshape(WIDTH, 256), preferred_element_type=F32)
            for d in (1, 2, 3):
                part = wov[d, :, :, :, :, cols].reshape(WIDTH, 256)
                total += jnp.dot(mx[d, rows, :], part, preferred_element_type=F32)
            out[rows, cols] = total.astype(BF16)
            return carry

        lax.fori_loop(0, 4, tile, 0)

    relay_out(0)
    direct_out(0)
    relay_out(1)
    merged_out(0)
    direct_out(1)
    relay_out(2)
    merged_out(1)
    direct_out(2)
    relay_out(3)
    attend(0)
    send_mixed(0)
    merged_out(2)
    direct_out(3)
    attend(1)
    send_mixed(1)
    merged_out(3)
    forward_mixed(0)
    attend(2)
    send_mixed(2)
    forward_mixed(1)
    attend(3)
    send_mixed(3)
    forward_mixed(2)
    wo_local.wait()
    wo_3.wait_recv()
    for i in range(NB):
        project(i)
    for copy in started:
        copy.wait_send()


def per_device(tokens, w_query, w_key, w_value, w_out, block_bucket):
    anywhere = pl.BlockSpec(memory_space=pl.ANY)
    dma = pltpu.SemaphoreType.DMA
    return pl.pallas_call(
        kernel,
        out_shape=jax.ShapeDtypeStruct((NB * BLK, FEAT), BF16),
        in_specs=[pl.BlockSpec(memory_space=pltpu.SMEM)] + [anywhere] * 5,
        out_specs=pl.BlockSpec(memory_space=pltpu.VMEM),
        scratch_shapes=[
            pltpu.VMEM((4, NB * BLK, FEAT), BF16),
            pltpu.VMEM((4, 3, FEAT, WIDTH), BF16),
            pltpu.VMEM((6, NB * BLK, 256), F32),
            pltpu.VMEM((2, NB, BLK, 256), BF16),
            pltpu.VMEM((2, 4, NB, BLK, PACK), BF16),
            pltpu.VMEM((2, 4, NB, BLK, PACK), BF16),
            pltpu.VMEM((2, NB, 6, HALF, PACK), BF16),
            pltpu.VMEM((2, NB, 2, HALF, PACK), BF16),
            pltpu.VMEM((2, 2, NB, BLK, PACK), BF16),
            pltpu.VMEM((2, BLK, PACK), BF16),
            pltpu.VMEM((4, 4, 4, 2, 16, FEAT), BF16),
            pltpu.VMEM((4, NB * BLK, WIDTH), BF16),
            pltpu.VMEM((3, 3, 8, 128), jnp.int32),
            pltpu.VMEM((3, 8, 128), jnp.int32),
            pltpu.VMEM((8, 128), jnp.int32),
            pltpu.SMEM((8, 128), jnp.int32),
            dma((3,)),
            dma((4, 3)),
            dma((2 * NB, 4)),
            dma((2 * NB, 4)),
            dma((3, 3)),
            dma((3, 3)),
            dma((2, NB, 7)),
            dma((2, NB, 7)),
            dma((2, NB, 6)),
            dma((2, NB, 6)),
            dma((16,)),
            dma((16,)),
            dma((NB, 4)),
            dma((NB, 4)),
        ],
        compiler_params=pltpu.CompilerParams(
            collective_id=0, has_side_effects=True, vmem_limit_bytes=58 * 2**20
        ),
    )(block_bucket, tokens, w_query, w_key, w_value, w_out)


def solution(mesh):
    placed = (
        P("seq", "head"),
        P(None, "head"),
        P(None, "head"),
        P(None, "head"),
        P("head", None),
        P("seq"),
    )
    return jax.shard_map(
        per_device, mesh=mesh, in_specs=placed, out_specs=P("seq", "head"), check_vma=False
    )
```

time: 109 us -> 97.5 us (0.89)
  Pallas kernels: 107 us -> 95.1 us
    pallas_call x1, Pallas kernels: 107 us -> 95.1 us  [per_device(): pl.pallas_call(kernel, out_shape=jax.ShapeDtypeStruct((NB * BLK, FEAT), B...]
where the time goes in v2:
time: 97.5 us; the launch traced here: 97.4 us
  Pallas kernels  95.1 us (98%)
  local copies, waits for them, and re-layouts  2.26 us (2%)
    pallas_call x1, Pallas kernels, per_device(): pl.pallas_call(kernel, out_shape=jax.ShapeDtypeStruct((NB * BLK, FEAT), B...  95.1 us
    unnamed x1, local copies, waits for them, and re-layouts  2.26 us

profile of v2, /device:TPU:1, one launch (start us, length us, event | category | flops | bytes accessed | tf_op | source)
XLA Modules:
  0.0 97.4 jit_solution(657151212499626877)
XLA Ops:
  0.0 95.1 %shard_map.64 = bf16[512,1024]{1,0:T(8,128)(2,1)} custom-call(s32[4]{0:T(128)} %ids.1, bf16[512,1024]{1,0:T(8,128)(2,1)} %tok.1, bf16[4096,512]{1,0:T(8,128)(2,1)} %wq.1, bf16[4096,512]{1,0:T(8,128)(2,1)} %wk.1, bf16[4096,512]{1,0:T(8,128)(2,1)} %wv.1, bf16[512,4096]{1,0:T(8,128)(2,1)} %wo.1), custom_call_target="tpu_custom_call" | custom-call | tf_op jit(solution)/shard_map/pallas_call | solution.py:402
  95.1 2.3 %copy.8 = bf16[512,1024]{1,0:T(8,128)(2,1)} copy(bf16[512,1024]{1,0:T(8,128)(2,1)} %shard_map.64) | data formatting | bytes 2097152

commit v3 on v2

--- a/solution.py
+++ b/solution.py
@@ -59,6 +59,10 @@
         started.append(copy)
         return copy
 
+    barrier = pltpu.get_barrier_semaphore()
+    for peer in peers:
+        pl.semaphore_signal(barrier, inc=1, device_id=peer, device_id_type=MESH)
+
     tok_local = pltpu.make_async_copy(tok, tk.at[0], loc_sem.at[0])
     tok_local.start()
     w_local = []
@@ -72,9 +76,6 @@
     wo_local = pltpu.make_async_copy(wo6.at[:, :, :, :, mine], wov.at[0], loc_sem.at[1])
     wo_local.start()
 
-    barrier = pltpu.get_barrier_semaphore()
-    for peer in peers:
-        pl.semaphore_signal(barrier, inc=1, device_id=peer, device_id_type=MESH)
     pl.semaphore_wait(barrier, len(peers))
 
     wo_y = []
@@ -94,11 +95,16 @@
     def tokens_event(k):
         lo, hi = pl.ds(k * HALF, HALF // 2), pl.ds(k * HALF + HALF // 2, HALF // 2)
         tok_c[k, 0].wait_recv()
-        tok_f[k, 0] = remote(tk.at[3, lo, :], tk.at[2, lo, :], tok_s.at[k, 2], tok_r.at[k, 2], ring("y", 1))
+        if k < 7:
+            tok_f[k, 0] = remote(tk.at[3, lo, :], tk.at[2, lo, :], tok_s.at[k, 2], tok_r.at[k, 2], ring("y", 1))
         tok_c[k, 1].wait_recv()
-        tok_f[k, 1] = remote(tk.at[1, hi, :], tk.at[2, hi, :], tok_s.at[k, 3], tok_r.at[k, 3], ring("y", -1))
+        if k < 7:
+            tok_f[k, 1] = remote(tk.at[1, hi, :], tk.at[2, hi, :], tok_s.at[k, 3], tok_r.at[k, 3], ring("y", -1))
         if k + 2 < 8:
             send_tokens(k + 2)
+        if k == 6:
+            rows = pl.ds(7 * HALF, HALF)
+            tok_f[7, 0] = remote(tok.at[rows, :], tk.at[2, rows, :], tok_s.at[7, 2], tok_r.at[7, 2], ring("y", 2))
 
     send_tokens(0)
     send_tokens(1)
@@ -144,8 +150,10 @@
 
         lax.fori_loop(0, 6, tile, 0)
 
-    def far_tiles(i, first, last):
-        rows = pl.ds(i * BLK, BLK)
+    pieces = ((0, 0, BLK), (1, 0, BLK), (2, 0, HALF), (2, HALF, HALF), (3, 0, HALF), (3, HALF, HALF))
+
+    def far_tiles(start, count, first, last):
+        rows = pl.ds(start, count)
 
         def tile(n, carry):
             cols = pl.ds(pl.multiple_of(lax.rem(n, 2) * 256, 256), 256)
@@ -157,34 +165,38 @@
     ag = {}
     axes = ("x", "z")
 
-    def finish_keys(i):
-        rows = pl.ds(i * BLK, BLK)
-        for k in (2 * i, 2 * i + 1):
+    def finish_keys(p):
+        i, start, count = pieces[p]
+        rows, part = pl.ds(i * BLK + start, count), pl.ds(start, count)
+        first = (i * BLK + start) // HALF
+        for k in range(first, first + count // HALF):
             tok_f[k, 0].wait_recv()
-            tok_f[k, 1].wait_recv()
-        far_tiles(i, 2, 6)
+            if k < 7:
+                tok_f[k, 1].wait_recv()
+        far_tiles(i * BLK + start, count, 2, 6)
         for f in range(2):
-            s1[f][0, 0, i, :, :256] = acc[2 + f, rows, :].astype(BF16)
-            s1[f][0, 0, i, :, 256:] = acc[4 + f, rows, :].astype(BF16)
+            s1[f][0, 0, i, part, :256] = acc[2 + f, rows, :].astype(BF16)
+            s1[f][0, 0, i, part, 256:] = acc[4 + f, rows, :].astype(BF16)
         for f in range(2):
-            own, a = s1[f].at[0, 0, i], axes[f]
+            own, a = s1[f].at[0, 0, i, part], axes[f]
             for n, (k, d) in enumerate(((2, 2), (1, 3), (-1, 1))):
-                ag[f, i, d] = remote(own, s1[f].at[0, d, i], ag_s.at[f, i, n], ag_r.at[f, i, n], ring(a, k))
-            ag[f, i, "own"] = remote(own, s1[f].at[1, 0, i], ag_s.at[f, i, 3], ag_r.at[f, i, 3], sibling)
+                ag[f, p, d] = remote(own, s1[f].at[0, d, i, part], ag_s.at[f, p, n], ag_r.at[f, p, n], ring(a, k))
+            ag[f, p, "own"] = remote(own, s1[f].at[1, 0, i, part], ag_s.at[f, p, 3], ag_r.at[f, p, 3], sibling)
 
     def finish_query(i):
         rows = pl.ds(i * BLK, BLK)
-        far_tiles(i, 0, 2)
+        far_tiles(i * BLK, BLK, 0, 2)
         for f in range(2):
             qs[f, i] = acc[f, rows, :].astype(BF16)
 
-    def to_sibling(i):
-        for n, d in ((0, 3), (1, 1), (2, 2)):
+    def to_sibling(p):
+        i, start, count = pieces[p]
+        part = pl.ds(start, count)
+        for n, d in ((2, 2), (0, 3), (1, 1)):
             for f in range(2):
-                ag[f, i, d].wait_recv()
-                ag[f, i, "s", d] = remote(
-                    s1[f].at[0, d, i], s1[f].at[1, d, i], ag_s.at[f, i, 4 + n], ag_r.at[f, i, 4 + n], sibling
-                )
+                ag[f, p, d].wait_recv()
+                src, dst = s1[f].at[0, d, i, part], s1[f].at[1, d, i, part]
+                ag[f, p, "s", d] = remote(src, dst, ag_s.at[f, p, 4 + n], ag_r.at[f, p, 4 + n], sibling)
 
     for copy in ids_x:
         copy.wait_recv()
@@ -247,19 +259,23 @@
     wo_3 = remote(own, own, wo_s.at[15], wo_r.at[15], sibling)
     tokens_event(5)
     near_tiles(2)
+    finish_keys(2)
     to_sibling(0)
     tokens_event(6)
     finish_query(1)
-    finish_keys(2)
+    finish_keys(3)
     tokens_event(7)
     near_tiles(3)
+    finish_keys(4)
+    finish_keys(5)
     to_sibling(1)
-    finish_keys(3)
+    to_sibling(2)
     finish_query(2)
-    to_sibling(2)
+    to_sibling(3)
     finish_query(3)
     part_copy.wait()
-    to_sibling(3)
+    to_sibling(4)
+    to_sibling(5)
 
     def choice(f, k, i):
         dest = place(x, wrap(z + k), c) if f == 0 else place(wrap(x + k), z, c)
@@ -273,10 +289,10 @@
     second = ("z", "x")
     here = (z, x)
     for f in range(2):
-        for i in range(NB):
-            ag[f, i, "own"].wait_recv()
+        for p in range(len(pieces)):
+            ag[f, p, "own"].wait_recv()
             for d in (1, 2, 3):
-                ag[f, i, "s", d].wait_recv()
+                ag[f, p, "s", d].wait_recv()
 
     low, high = pl.ds(0, HALF), pl.ds(HALF, HALF)
     rs = {}
@@ -306,12 +322,12 @@
             rs[f, i, 1].wait_recv()
             pass_on(f, i, 5, -1, high, -1, fin.at[f, 1, i, high], 1)
 
-    def attend(i):
+    def attend(i, halves=(0, 1)):
         rows = pl.ds(i * BLK, BLK)
-        for f in range(2):
+        for f in halves:
             for g in (2, 3, 4, 5):
                 rs[f, i, g].wait_recv()
-        for f in range(2):
+        for f in halves:
             index, held, p = choice(f, 0, i)
             at_left, at_right = held == wrap(here[f] - 1), held == wrap(here[f] + 1)
             for half, from_left in ((low, jnp.logical_not(at_right)), (high, at_left)):
@@ -337,10 +353,14 @@
 
     def send_mixed(i):
         rows = pl.ds(i * BLK, BLK)
-        if i == NB - 1:
-            mx_c[i, 2] = remote(mx.at[0, rows], mx.at[2, rows], mx_s.at[i, 2], mx_r.at[i, 2], ring("y", 2))
         mx_c[i, 0] = remote(mx.at[0, rows], mx.at[3, rows], mx_s.at[i, 0], mx_r.at[i, 0], ring("y", 1))
         mx_c[i, 1] = remote(mx.at[0, rows], mx.at[1, rows], mx_s.at[i, 1], mx_r.at[i, 1], ring("y", -1))
+
+    def send_last(f):
+        part = (pl.ds((NB - 1) * BLK, BLK), pl.ds(f * 256, 256))
+        for n, (k, d) in enumerate(((2, 2), (1, 3), (-1, 1))):
+            at = NB - 1 + f, n
+            mx_c["last", f, d] = remote(mx.at[(0, *part)], mx.at[(d, *part)], mx_s.at[at], mx_r.at[at], ring("y", k))
 
     def forward_mixed(i):
         lo, hi = pl.ds(i * BLK, HALF), pl.ds(i * BLK + HALF, HALF)
@@ -351,7 +371,7 @@
 
     def project(i):
         rows = pl.ds(i * BLK, BLK)
-        for n in (0, 1, 2) if i == NB - 1 else (2, 3):
+        for n in (2, 3):
             mx_c[i, n].wait_recv()
 
         def tile(n, carry):
@@ -365,6 +385,27 @@
 
         lax.fori_loop(0, 4, tile, 0)
 
+    def project_last(steps, store):
+        rows = pl.ds((NB - 1) * BLK, BLK)
+
+        def tile(n, carry):
+            cols = pl.ds(pl.multiple_of(n * 256, 256), 256)
+            total = jnp.zeros((BLK, 256), F32) if 0 in steps else acc[n, pl.ds(0, BLK), :]
+            for d in steps:
+                part = wov[d, :, :, :, :, cols].reshape(WIDTH, 256)
+                total += jnp.dot(mx[d, rows, :], part, preferred_element_type=F32)
+            if store:
+                out[rows, cols] = total.astype(BF16)
+            else:
+                acc[n, pl.ds(0, BLK), :] = total
+            return carry
+
+        for d in steps:
+            for f in range(2) if d else ():
+                mx_c["last", f, d].wait_recv()
+        lax.fori_loop(0, 4, tile, 0)
+
+    before_exchange = len(started)
     relay_out(0)
     direct_out(0)
     relay_out(1)
@@ -385,14 +426,24 @@
     attend(2)
     send_mixed(2)
     forward_mixed(1)
-    attend(3)
-    send_mixed(3)
+    attend(3, (0,))
+    send_last(0)
+    attend(3, (1,))
+    send_last(1)
     forward_mixed(2)
     wo_local.wait()
     wo_3.wait_recv()
-    for i in range(NB):
-        project(i)
-    for copy in started:
+    for copy in started[:before_exchange]:
+        copy.wait_send()
+    project(0)
+    for copy in rs.values():
+        copy.wait_send()
+    project(1)
+    project_last((0,), False)
+    project(2)
+    project_last((2,), False)
+    project_last((3, 1), True)
+    for copy in mx_c.values():
         copy.wait_send()
 
 
@@ -427,14 +478,14 @@
             dma((2 * NB, 4)),
             dma((3, 3)),
             dma((3, 3)),
-            dma((2, NB, 7)),
-            dma((2, NB, 7)),
+            dma((2, NB + 2, 7)),
+            dma((2, NB + 2, 7)),
             dma((2, NB, 6)),
             dma((2, NB, 6)),
             dma((16,)),
             dma((16,)),
-            dma((NB, 4)),
-            dma((NB, 4)),
+            dma((NB + 1, 4)),
+            dma((NB + 1, 4)),
         ],
         compiler_params=pltpu.CompilerParams(
             collective_id=0, has_side_effects=True, vmem_limit_bytes=58 * 2**20

time: 97.5 us -> 97 us (level)
  no operation moved by 1% of the time
where the time goes in v3:
time: 97 us; the launch traced here: 96.9 us
  Pallas kernels  94.6 us (98%)
  local copies, waits for them, and re-layouts  2.26 us (2%)
    pallas_call x1, Pallas kernels, per_device(): pl.pallas_call(kernel, out_shape=jax.ShapeDtypeStruct((NB * BLK, FEAT), B...  94.6 us
    unnamed x1, local copies, waits for them, and re-layouts  2.26 us

profile of v3, /device:TPU:1, one launch (start us, length us, event | category | flops | bytes accessed | tf_op | source)
XLA Modules:
  0.0 96.9 jit_solution(16526646482420463807)
XLA Ops:
  0.0 94.6 %shard_map.64 = bf16[512,1024]{1,0:T(8,128)(2,1)} custom-call(s32[4]{0:T(128)} %ids.1, bf16[512,1024]{1,0:T(8,128)(2,1)} %tok.1, bf16[4096,512]{1,0:T(8,128)(2,1)} %wq.1, bf16[4096,512]{1,0:T(8,128)(2,1)} %wk.1, bf16[4096,512]{1,0:T(8,128)(2,1)} %wv.1, bf16[512,4096]{1,0:T(8,128)(2,1)} %wo.1), custom_call_target="tpu_custom_call" | custom-call | tf_op jit(solution)/shard_map/pallas_call | solution.py:453
  94.6 2.3 %copy.8 = bf16[512,1024]{1,0:T(8,128)(2,1)} copy(bf16[512,1024]{1,0:T(8,128)(2,1)} %shard_map.64) | data formatting | bytes 2097152

commit v4 on v3

--- a/solution.py
+++ b/solution.py
@@ -452,7 +452,7 @@
     dma = pltpu.SemaphoreType.DMA
     return pl.pallas_call(
         kernel,
-        out_shape=jax.ShapeDtypeStruct((NB * BLK, FEAT), BF16),
+        out_shape=pltpu.VMEM((NB * BLK, FEAT), BF16),
         in_specs=[pl.BlockSpec(memory_space=pltpu.SMEM)] + [anywhere] * 5,
         out_specs=pl.BlockSpec(memory_space=pltpu.VMEM),
         scratch_shapes=[

time: 97 us -> 94.7 us (0.976)
  local copies, waits for them, and re-layouts: 2.26 us -> 0.97 us
  Pallas kernels: 94.6 us -> 93.6 us
    unnamed x1, local copies, waits for them, and re-layouts: 2.26 us -> 0.97 us
    pallas_call x1, Pallas kernels: 94.6 us -> 93.6 us  [per_device(): pl.pallas_call(kernel, out_shape=pltpu.VMEM((NB * BLK, FEAT), BF16), in_s...]
where the time goes in v4:
time: 94.7 us; the launch traced here: 94.6 us
  Pallas kernels  93.6 us (99%)
  local copies, waits for them, and re-layouts  0.97 us (1%)
    pallas_call x1, Pallas kernels, per_device(): pl.pallas_call(kernel, out_shape=pltpu.VMEM((NB * BLK, FEAT), BF16), in_s...  93.6 us

profile of v4, /device:TPU:1, one launch (start us, length us, event | category | flops | bytes accessed | tf_op | source)
XLA Modules:
  0.0 94.6 jit_solution(5932550667500313974)
XLA Ops:
  0.0 93.6 %shard_map.64 = bf16[512,1024]{1,0:T(8,128)(2,1)S(1)} custom-call(s32[4]{0:T(128)} %ids.1, bf16[512,1024]{1,0:T(8,128)(2,1)} %tok.1, bf16[4096,512]{1,0:T(8,128)(2,1)} %wq.1, bf16[4096,512]{1,0:T(8,128)(2,1)} %wk.1, bf16[4096,512]{1,0:T(8,128)(2,1)} %wv.1, bf16[512,4096]{1,0:T(8,128)(2,1)} %wo.1), custom_call_target="tpu_custom_call" | custom-call | tf_op jit(solution)/shard_map/pallas_call | solution.py:453
  93.6 1.0 %copy.8 = bf16[512,1024]{1,0:T(8,128)(2,1)} copy(bf16[512,1024]{1,0:T(8,128)(2,1)S(1)} %shard_map.64) | data formatting | bytes 2097152

commit v5 on v4

--- a/solution.py
+++ b/solution.py
@@ -13,6 +13,7 @@
 FEAT = 1024
 WIDTH = 512
 PACK = 512
+UNIT = 256
 MESH = pl.DeviceIdType.MESH
 F32 = jnp.float32
 BF16 = jnp.bfloat16
@@ -34,6 +35,7 @@
     z = lax.rem(s // 2, 4)
     c = lax.rem(s, 2)
     s1 = (s1a, s1b)
+    px = lax.rem(x, 2) * 2 + x // 2
     wo6 = wo.reshape(4, 4, 2, 16, 4 * FEAT)
     started = []
 
@@ -73,8 +75,12 @@
             copy.start()
             w_local.append(copy)
     mine = pl.ds(pl.multiple_of(y * FEAT, FEAT), FEAT)
-    wo_local = pltpu.make_async_copy(wo6.at[:, :, :, :, mine], wov.at[0], loc_sem.at[1])
-    wo_local.start()
+    wo_local = []
+    for h in range(4):
+        src, dst = wo6.at[h, :, :, :, mine], wov.at[0, h % 2 * 2 + h // 2]
+        wo_local.append(pltpu.make_async_copy(src, dst, loc_sem.at[3 + h]))
+    for copy in wo_local:
+        copy.start()
 
     pl.semaphore_wait(barrier, len(peers))
 
@@ -82,7 +88,7 @@
     row16 = pl.ds(pl.multiple_of(s * 16, 16), 16)
     for k in (1, 2, 3):
         cols = pl.ds(pl.multiple_of(wrap(y + k) * FEAT, FEAT), FEAT)
-        wo_y.append(remote(wo.at[row16, cols], wov.at[4 - k, x, z, c], wo_s.at[k - 1], wo_r.at[k - 1], ring("y", k)))
+        wo_y.append(remote(wo.at[row16, cols], wov.at[4 - k, px, z, c], wo_s.at[k - 1], wo_r.at[k - 1], ring("y", k)))
 
     tok_c = {}
     tok_f = {}
@@ -175,8 +181,10 @@
                 tok_f[k, 1].wait_recv()
         far_tiles(i * BLK + start, count, 2, 6)
         for f in range(2):
-            s1[f][0, 0, i, part, :256] = acc[2 + f, rows, :].astype(BF16)
-            s1[f][0, 0, i, part, 256:] = acc[4 + f, rows, :].astype(BF16)
+            for j in range(2):
+                head = pl.ds(j * HDIM, HDIM)
+                s1[f][0, 0, i, part, pl.ds(j * 256, HDIM)] = acc[2 + f, rows, head].astype(BF16)
+                s1[f][0, 0, i, part, pl.ds(j * 256 + HDIM, HDIM)] = acc[4 + f, rows, head].astype(BF16)
         for f in range(2):
             own, a = s1[f].at[0, 0, i, part], axes[f]
             for n, (k, d) in enumerate(((2, 2), (1, 3), (-1, 1))):
@@ -209,9 +217,9 @@
     three = pl.ds(1, 3)
     wo_1 = []
     for k in (2, 1, 3):
-        own = wov.at[three, x, z, c, :, left_cols]
+        own = wov.at[three, px, z, c, :, left_cols]
         wo_1.append(remote(own, own, wo_s.at[2 + k], wo_r.at[2 + k], ring("x", k)))
-        own = wov.at[three, x, z, c, :, right_cols]
+        own = wov.at[three, px, z, c, :, right_cols]
         wo_1.append(remote(own, own, wo_s.at[5 + k], wo_r.at[5 + k], ring("z", k)))
 
     tokens_event(0)
@@ -229,7 +237,7 @@
     for k in (2, 1, 3):
         own = wov.at[three, :, z, c, :, left_cols]
         wo_2.append(remote(own, own, wo_s.at[8 + k], wo_r.at[8 + k], ring("z", k)))
-        own = wov.at[three, x, :, c, :, right_cols]
+        own = wov.at[three, px, :, c, :, right_cols]
         wo_2.append(remote(own, own, wo_s.at[11 + k], wo_r.at[11 + k], ring("x", k)))
 
     near_tiles(0)
@@ -296,153 +304,164 @@
 
     low, high = pl.ds(0, HALF), pl.ds(HALF, HALF)
     rs = {}
-
-    def pass_on(f, i, g, k, rows, to, dst, relay=None):
-        index, held, _ = choice(f, k, i)
-        packet = s1[f][index[0], index[1], index[2], rows]
+    choices = {}
+
+    def chosen(f, k, i):
+        if (f, k, i) not in choices:
+            choices[f, k, i] = choice(f, k, i)
+        return choices[f, k, i]
+
+    def pass_on(f, u, g, k, rows, to, dst, relay=None):
+        i, j = divmod(u, 2)
+        index, held, _ = chosen(f, k, i)
+        packet = s1[f][index[0], index[1], index[2], rows, pl.ds(j * UNIT, UNIT)]
         if relay is not None:
-            packet = jnp.where(held == here[f], packet, rel[f, i, relay])
-        tx[f, i, g] = packet
-        rs[f, i, g] = remote(tx.at[f, i, g], dst, rs_s.at[f, i, g], rs_r.at[f, i, g], ring(second[f], to))
-
-    def relay_out(i):
-        for f in range(2):
-            pass_on(f, i, 0, 2, low, 1, rel.at[f, i, 0])
-            pass_on(f, i, 1, 2, high, -1, rel.at[f, i, 1])
-
-    def direct_out(i):
-        for f in range(2):
-            pass_on(f, i, 2, 1, high, 1, fin.at[f, 0, i, high])
-            pass_on(f, i, 3, -1, low, -1, fin.at[f, 1, i, low])
-
-    def merged_out(i):
-        for f in range(2):
-            rs[f, i, 0].wait_recv()
-            pass_on(f, i, 4, 1, low, 1, fin.at[f, 0, i, low], 0)
-            rs[f, i, 1].wait_recv()
-            pass_on(f, i, 5, -1, high, -1, fin.at[f, 1, i, high], 1)
-
-    def attend(i, halves=(0, 1)):
+            packet = jnp.where(held == here[f], packet, rel[f, u, relay])
+        tx[f, u, g] = packet
+        rs[f, u, g] = remote(tx.at[f, u, g], dst, rs_s.at[f, u, g], rs_r.at[f, u, g], ring(second[f], to))
+
+    def relay_out(u):
+        for f in range(2):
+            pass_on(f, u, 0, 2, low, 1, rel.at[f, u, 0])
+            pass_on(f, u, 1, 2, high, -1, rel.at[f, u, 1])
+
+    def direct_out(u):
+        for f in range(2):
+            pass_on(f, u, 2, 1, high, 1, fin.at[f, 0, u, high])
+            pass_on(f, u, 3, -1, low, -1, fin.at[f, 1, u, low])
+
+    def merged_out(u):
+        for f in range(2):
+            rs[f, u, 0].wait_recv()
+            pass_on(f, u, 4, 1, low, 1, fin.at[f, 0, u, low], 0)
+            rs[f, u, 1].wait_recv()
+            pass_on(f, u, 5, -1, high, -1, fin.at[f, 1, u, high], 1)
+
+    mx_c = {}
+
+    def send_mixed(u):
+        i, j = divmod(u, 2)
         rows = pl.ds(i * BLK, BLK)
-        for f in halves:
+        own = mx.at[0, j, rows]
+        if u == 7:
+            mx_c[u, 2] = remote(own, mx.at[2, j, rows], mx_s.at[u, 2], mx_r.at[u, 2], ring("y", 2))
+        mx_c[u, 0] = remote(own, mx.at[3, j, rows], mx_s.at[u, 0], mx_r.at[u, 0], ring("y", 1))
+        mx_c[u, 1] = remote(own, mx.at[1, j, rows], mx_s.at[u, 1], mx_r.at[u, 1], ring("y", -1))
+
+    def forward_mixed(u):
+        i, j = divmod(u, 2)
+        lo, hi = pl.ds(i * BLK, HALF), pl.ds(i * BLK + HALF, HALF)
+        mx_c[u, 0].wait_recv()
+        mx_c[u, 2] = remote(mx.at[3, j, lo], mx.at[2, j, lo], mx_s.at[u, 2], mx_r.at[u, 2], ring("y", 1))
+        mx_c[u, 1].wait_recv()
+        mx_c[u, 3] = remote(mx.at[1, j, hi], mx.at[2, j, hi], mx_s.at[u, 3], mx_r.at[u, 3], ring("y", -1))
+
+    def attend(u):
+        i, j = divmod(u, 2)
+        rows = pl.ds(i * BLK, BLK)
+        for f in range(2):
             for g in (2, 3, 4, 5):
-                rs[f, i, g].wait_recv()
-        for f in halves:
-            index, held, p = choice(f, 0, i)
+                rs[f, u, g].wait_recv()
+        kc, vc = pl.ds(j * UNIT, HDIM), pl.ds(j * UNIT + HDIM, HDIM)
+        for f in range(2):
+            index, held, p = chosen(f, 0, i)
             at_left, at_right = held == wrap(here[f] - 1), held == wrap(here[f] + 1)
             for half, from_left in ((low, jnp.logical_not(at_right)), (high, at_left)):
-                packet = jnp.where(from_left, fin[f, 0, i, half], fin[f, 1, i, half])
-                own = s1[f][index[0], index[1], index[2], half]
+                packet = jnp.where(from_left, fin[f, 0, u, half], fin[f, 1, u, half])
+                own = s1[f][index[0], index[1], index[2], half, pl.ds(j * UNIT, UNIT)]
                 kvp[f, half] = jnp.where(held == here[f], own, packet)
-            for j in range(2):
-                kc, vc = pl.ds(j * HDIM, HDIM), pl.ds(256 + j * HDIM, HDIM)
-                query = qs[f, i, :, kc]
-                dims = (((1,), (1,)), ((), ()))
-                near = lax.dot_general(query, s1[f][0, 0, i, :, kc], dims, preferred_element_type=F32) * SCALE
-                far = lax.dot_general(query, kvp[f, :, kc], dims, preferred_element_type=F32) * SCALE
-                far = jnp.where(p >= 0, far, -1e30)
-                top = jnp.maximum(jnp.max(near, axis=1, keepdims=True), jnp.max(far, axis=1, keepdims=True))
-                near, far = jnp.exp(near - top), jnp.exp(far - top)
-                total = jnp.sum(near, axis=1, keepdims=True) + jnp.sum(far, axis=1, keepdims=True)
-                near, far = (near / total).astype(BF16), (far / total).astype(BF16)
-                mixed = jnp.dot(near, s1[f][0, 0, i, :, vc], preferred_element_type=F32)
-                mixed += jnp.dot(far, kvp[f, :, vc], preferred_element_type=F32)
-                mx[0, rows, pl.ds((2 * f + j) * HDIM, HDIM)] = mixed.astype(BF16)
-
-    mx_c = {}
-
-    def send_mixed(i):
+            query = qs[f, i, :, pl.ds(j * HDIM, HDIM)]
+            dims = (((1,), (1,)), ((), ()))
+            near = lax.dot_general(query, s1[f][0, 0, i, :, kc], dims, preferred_element_type=F32) * SCALE
+            far = lax.dot_general(query, kvp[f, :, :HDIM], dims, preferred_element_type=F32) * SCALE
+            far = jnp.where(p >= 0, far, -1e30)
+            top = jnp.maximum(jnp.max(near, axis=1, keepdims=True), jnp.max(far, axis=1, keepdims=True))
+            near, far = jnp.exp(near - top), jnp.exp(far - top)
+            total = jnp.sum(near, axis=1, keepdims=True) + jnp.sum(far, axis=1, keepdims=True)
+            near, far = (near / total).astype(BF16), (far / total).astype(BF16)
+            mixed = jnp.dot(near, s1[f][0, 0, i, :, vc], preferred_element_type=F32)
+            mixed += jnp.dot(far, kvp[f, :, HDIM:], preferred_element_type=F32)
+            mx[0, j, rows, pl.ds(f * HDIM, HDIM)] = mixed.astype(BF16)
+        send_mixed(u)
+
+    def project(i, steps, first=True, last=True):
         rows = pl.ds(i * BLK, BLK)
-        mx_c[i, 0] = remote(mx.at[0, rows], mx.at[3, rows], mx_s.at[i, 0], mx_r.at[i, 0], ring("y", 1))
-        mx_c[i, 1] = remote(mx.at[0, rows], mx.at[1, rows], mx_s.at[i, 1], mx_r.at[i, 1], ring("y", -1))
-
-    def send_last(f):
-        part = (pl.ds((NB - 1) * BLK, BLK), pl.ds(f * 256, 256))
-        for n, (k, d) in enumerate(((2, 2), (1, 3), (-1, 1))):
-            at = NB - 1 + f, n
-            mx_c["last", f, d] = remote(mx.at[(0, *part)], mx.at[(d, *part)], mx_s.at[at], mx_r.at[at], ring("y", k))
-
-    def forward_mixed(i):
-        lo, hi = pl.ds(i * BLK, HALF), pl.ds(i * BLK + HALF, HALF)
-        mx_c[i, 0].wait_recv()
-        mx_c[i, 2] = remote(mx.at[3, lo], mx.at[2, lo], mx_s.at[i, 2], mx_r.at[i, 2], ring("y", 1))
-        mx_c[i, 1].wait_recv()
-        mx_c[i, 3] = remote(mx.at[1, hi], mx.at[2, hi], mx_s.at[i, 3], mx_r.at[i, 3], ring("y", -1))
-
-    def project(i):
-        rows = pl.ds(i * BLK, BLK)
-        for n in (2, 3):
-            mx_c[i, n].wait_recv()
 
         def tile(n, carry):
             cols = pl.ds(pl.multiple_of(n * 256, 256), 256)
-            total = jnp.dot(mx[0, rows, :], wov[0, :, :, :, :, cols].reshape(WIDTH, 256), preferred_element_type=F32)
-            for d in (1, 2, 3):
-                part = wov[d, :, :, :, :, cols].reshape(WIDTH, 256)
-                total += jnp.dot(mx[d, rows, :], part, preferred_element_type=F32)
-            out[rows, cols] = total.astype(BF16)
-            return carry
-
-        lax.fori_loop(0, 4, tile, 0)
-
-    def project_last(steps, store):
-        rows = pl.ds((NB - 1) * BLK, BLK)
-
-        def tile(n, carry):
-            cols = pl.ds(pl.multiple_of(n * 256, 256), 256)
-            total = jnp.zeros((BLK, 256), F32) if 0 in steps else acc[n, pl.ds(0, BLK), :]
-            for d in steps:
-                part = wov[d, :, :, :, :, cols].reshape(WIDTH, 256)
-                total += jnp.dot(mx[d, rows, :], part, preferred_element_type=F32)
-            if store:
+            total = jnp.zeros((BLK, 256), F32) if first else acc[n, pl.ds(0, BLK), :]
+            for d, j in steps:
+                part = wov[d, pl.ds(2 * j, 2), :, :, :, cols].reshape(256, 256)
+                total += jnp.dot(mx[d, j, rows, :], part, preferred_element_type=F32)
+            if last:
                 out[rows, cols] = total.astype(BF16)
             else:
                 acc[n, pl.ds(0, BLK), :] = total
             return carry
 
-        for d in steps:
-            for f in range(2) if d else ():
-                mx_c["last", f, d].wait_recv()
         lax.fori_loop(0, 4, tile, 0)
 
+    def arrived(*units):
+        for u in units:
+            for n in (0, 1, 2) if u == 7 else (2, 3):
+                mx_c[u, n].wait_recv()
+
     before_exchange = len(started)
-    relay_out(0)
-    direct_out(0)
-    relay_out(1)
+    for u in (0, 1, 2):
+        relay_out(u)
+        direct_out(u)
     merged_out(0)
-    direct_out(1)
-    relay_out(2)
+    relay_out(3)
+    direct_out(3)
     merged_out(1)
-    direct_out(2)
-    relay_out(3)
+    relay_out(4)
+    relay_out(5)
+    merged_out(2)
+    direct_out(4)
+    relay_out(6)
     attend(0)
-    send_mixed(0)
-    merged_out(2)
-    direct_out(3)
+    merged_out(3)
+    direct_out(5)
+    relay_out(7)
     attend(1)
-    send_mixed(1)
-    merged_out(3)
+    merged_out(4)
+    direct_out(6)
+    merged_out(5)
+    direct_out(7)
+    attend(2)
     forward_mixed(0)
-    attend(2)
-    send_mixed(2)
+    merged_out(6)
+    attend(3)
     forward_mixed(1)
-    attend(3, (0,))
-    send_last(0)
-    attend(3, (1,))
-    send_last(1)
+    merged_out(7)
+    attend(4)
     forward_mixed(2)
-    wo_local.wait()
+    attend(5)
+    attend(6)
+    forward_mixed(3)
+    attend(7)
+    forward_mixed(4)
+    forward_mixed(5)
+    for copy in wo_local:
+        copy.wait()
     wo_3.wait_recv()
+    every = [(d, j) for d in range(4) for j in range(2)]
+    arrived(0, 1)
+    project(0, every)
+    forward_mixed(6)
     for copy in started[:before_exchange]:
         copy.wait_send()
-    project(0)
+    project(3, every[:2], True, False)
+    arrived(2, 3)
+    project(1, every)
     for copy in rs.values():
         copy.wait_send()
-    project(1)
-    project_last((0,), False)
-    project(2)
-    project_last((2,), False)
-    project_last((3, 1), True)
+    arrived(4, 5)
+    project(2, every)
+    arrived(6)
+    project(3, [(d, 0) for d in (1, 2, 3)], False, False)
+    arrived(7)
+    project(3, [(d, 1) for d in (1, 2, 3)], False, True)
     for copy in mx_c.values():
         copy.wait_send()
 
@@ -462,17 +481,17 @@
             pltpu.VMEM((2, NB, BLK, 256), BF16),
             pltpu.VMEM((2, 4, NB, BLK, PACK), BF16),
             pltpu.VMEM((2, 4, NB, BLK, PACK), BF16),
-            pltpu.VMEM((2, NB, 6, HALF, PACK), BF16),
-            pltpu.VMEM((2, NB, 2, HALF, PACK), BF16),
-            pltpu.VMEM((2, 2, NB, BLK, PACK), BF16),
-            pltpu.VMEM((2, BLK, PACK), BF16),
+            pltpu.VMEM((2, 2 * NB, 6, HALF, UNIT), BF16),
+            pltpu.VMEM((2, 2 * NB, 2, HALF, UNIT), BF16),
+            pltpu.VMEM((2, 2, 2 * NB, BLK, UNIT), BF16),
+            pltpu.VMEM((2, BLK, UNIT), BF16),
             pltpu.VMEM((4, 4, 4, 2, 16, FEAT), BF16),
-            pltpu.VMEM((4, NB * BLK, WIDTH), BF16),
+            pltpu.VMEM((4, 2, NB * BLK, 256), BF16),
             pltpu.VMEM((3, 3, 8, 128), jnp.int32),
             pltpu.VMEM((3, 8, 128), jnp.int32),
             pltpu.VMEM((8, 128), jnp.int32),
             pltpu.SMEM((8, 128), jnp.int32),
-            dma((3,)),
+            dma((7,)),
             dma((4, 3)),
             dma((2 * NB, 4)),
             dma((2 * NB, 4)),
@@ -480,12 +499,12 @@
             dma((3, 3)),
             dma((2, NB + 2, 7)),
             dma((2, NB + 2, 7)),
-            dma((2, NB, 6)),
-            dma((2, NB, 6)),
+            dma((2, 2 * NB, 6)),
+            dma((2, 2 * NB, 6)),
             dma((16,)),
             dma((16,)),
-            dma((NB + 1, 4)),
-            dma((NB + 1, 4)),
+            dma((2 * NB, 4)),
+            dma((2 * NB, 4)),
         ],
         compiler_params=pltpu.CompilerParams(
             collective_id=0, has_side_effects=True, vmem_limit_bytes=58 * 2**20

time: 94.7 us -> 93 us (0.982)
  Pallas kernels: 93.6 us -> 91.9 us
    pallas_call x1, Pallas kernels: 93.6 us -> 91.9 us  [per_device(): pl.pallas_call(kernel, out_shape=pltpu.VMEM((NB * BLK, FEAT), BF16), in_s...]
where the time goes in v5:
time: 93 us; the launch traced here: 92.9 us
  Pallas kernels  91.9 us (99%)
  local copies, waits for them, and re-layouts  0.97 us (1%)
    pallas_call x1, Pallas kernels, per_device(): pl.pallas_call(kernel, out_shape=pltpu.VMEM((NB * BLK, FEAT), BF16), in_s...  91.9 us

profile of v5, /device:TPU:1, one launch (start us, length us, event | category | flops | bytes accessed | tf_op | source)
XLA Modules:
  0.0 92.9 jit_solution(12080358988820853789)
XLA Ops:
  0.0 91.9 %shard_map.64 = bf16[512,1024]{1,0:T(8,128)(2,1)S(1)} custom-call(s32[4]{0:T(128)} %ids.1, bf16[512,1024]{1,0:T(8,128)(2,1)} %tok.1, bf16[4096,512]{1,0:T(8,128)(2,1)} %wq.1, bf16[4096,512]{1,0:T(8,128)(2,1)} %wk.1, bf16[4096,512]{1,0:T(8,128)(2,1)} %wv.1, bf16[512,4096]{1,0:T(8,128)(2,1)} %wo.1), custom_call_target="tpu_custom_call" | custom-call | tf_op jit(solution)/shard_map/pallas_call | solution.py:472
  91.9 1.0 %copy.8 = bf16[512,1024]{1,0:T(8,128)(2,1)} copy(bf16[512,1024]{1,0:T(8,128)(2,1)S(1)} %shard_map.64) | data formatting | bytes 2097152

commit v6 on v5

--- a/solution.py
+++ b/solution.py
@@ -384,19 +384,19 @@
             mx[0, j, rows, pl.ds(f * HDIM, HDIM)] = mixed.astype(BF16)
         send_mixed(u)
 
-    def project(i, steps, first=True, last=True):
-        rows = pl.ds(i * BLK, BLK)
+    def project(start, count, steps, first=True, last=True):
+        rows = pl.ds(start, count)
 
         def tile(n, carry):
             cols = pl.ds(pl.multiple_of(n * 256, 256), 256)
-            total = jnp.zeros((BLK, 256), F32) if first else acc[n, pl.ds(0, BLK), :]
+            total = jnp.zeros((count, 256), F32) if first else acc[n, rows, :]
             for d, j in steps:
                 part = wov[d, pl.ds(2 * j, 2), :, :, :, cols].reshape(256, 256)
                 total += jnp.dot(mx[d, j, rows, :], part, preferred_element_type=F32)
             if last:
                 out[rows, cols] = total.astype(BF16)
             else:
-                acc[n, pl.ds(0, BLK), :] = total
+                acc[n, rows, :] = total
             return carry
 
         lax.fori_loop(0, 4, tile, 0)
@@ -407,38 +407,43 @@
                 mx_c[u, n].wait_recv()
 
     before_exchange = len(started)
-    for u in (0, 1, 2):
-        relay_out(u)
-        direct_out(u)
+    relay_out(0)
+    relay_out(1)
+    direct_out(0)
+    direct_out(1)
+    relay_out(2)
+    for copy in started[:before_exchange]:
+        copy.wait_send()
     merged_out(0)
+    merged_out(1)
+    direct_out(2)
     relay_out(3)
     direct_out(3)
-    merged_out(1)
+    merged_out(2)
     relay_out(4)
     relay_out(5)
-    merged_out(2)
+    attend(0)
+    attend(1)
+    merged_out(3)
     direct_out(4)
     relay_out(6)
-    attend(0)
-    merged_out(3)
+    attend(2)
+    merged_out(4)
     direct_out(5)
     relay_out(7)
-    attend(1)
-    merged_out(4)
+    forward_mixed(0)
+    merged_out(5)
     direct_out(6)
-    merged_out(5)
-    direct_out(7)
-    attend(2)
-    forward_mixed(0)
-    merged_out(6)
     attend(3)
     forward_mixed(1)
+    merged_out(6)
+    attend(4)
+    direct_out(7)
     merged_out(7)
-    attend(4)
     forward_mixed(2)
     attend(5)
+    forward_mixed(3)
     attend(6)
-    forward_mixed(3)
     attend(7)
     forward_mixed(4)
     forward_mixed(5)
@@ -446,22 +451,18 @@
         copy.wait()
     wo_3.wait_recv()
     every = [(d, j) for d in range(4) for j in range(2)]
-    arrived(0, 1)
-    project(0, every)
+    arrived(0, 1, 2, 3)
+    project(0, 256, every)
     forward_mixed(6)
-    for copy in started[:before_exchange]:
-        copy.wait_send()
-    project(3, every[:2], True, False)
-    arrived(2, 3)
-    project(1, every)
+    project(256, 256, [(0, 0), (0, 1), (3, 0), (1, 0)], True, False)
     for copy in rs.values():
         copy.wait_send()
+    arrived(7)
+    project(256, 256, [(3, 1), (1, 1)], False, False)
     arrived(4, 5)
-    project(2, every)
+    project(256, 128, [(2, 0), (2, 1)], False, True)
     arrived(6)
-    project(3, [(d, 0) for d in (1, 2, 3)], False, False)
-    arrived(7)
-    project(3, [(d, 1) for d in (1, 2, 3)], False, True)
+    project(384, 128, [(2, 0), (2, 1)], False, True)
     for copy in mx_c.values():
         copy.wait_send()
 

time: 93 us -> 90.3 us (0.971)
  Pallas kernels: 91.9 us -> 89.2 us
    pallas_call x1, Pallas kernels: 91.9 us -> 89.2 us  [per_device(): pl.pallas_call(kernel, out_shape=pltpu.VMEM((NB * BLK, FEAT), BF16), in_s...]
where the time goes in v6:
time: 90.3 us; the launch traced here: 90.2 us
  Pallas kernels  89.2 us (99%)
  local copies, waits for them, and re-layouts  0.97 us (1%)
    pallas_call x1, Pallas kernels, per_device(): pl.pallas_call(kernel, out_shape=pltpu.VMEM((NB * BLK, FEAT), BF16), in_s...  89.2 us

profile of v6, /device:TPU:1, one launch (start us, length us, event | category | flops | bytes accessed | tf_op | source)
XLA Modules:
  0.0 90.2 jit_solution(4530139356511880984)
XLA Ops:
  0.0 89.2 %shard_map.64 = bf16[512,1024]{1,0:T(8,128)(2,1)S(1)} custom-call(s32[4]{0:T(128)} %ids.1, bf16[512,1024]{1,0:T(8,128)(2,1)} %tok.1, bf16[4096,512]{1,0:T(8,128)(2,1)} %wq.1, bf16[4096,512]{1,0:T(8,128)(2,1)} %wk.1, bf16[4096,512]{1,0:T(8,128)(2,1)} %wv.1, bf16[512,4096]{1,0:T(8,128)(2,1)} %wo.1), custom_call_target="tpu_custom_call" | custom-call | tf_op jit(solution)/shard_map/pallas_call | solution.py:473
  89.2 1.0 %copy.8 = bf16[512,1024]{1,0:T(8,128)(2,1)} copy(bf16[512,1024]{1,0:T(8,128)(2,1)S(1)} %shard_map.64) | data formatting | bytes 2097152

commit v7 on v6

--- a/solution.py
+++ b/solution.py
@@ -421,8 +421,8 @@
     direct_out(3)
     merged_out(2)
     relay_out(4)
+    attend(0)
     relay_out(5)
-    attend(0)
     attend(1)
     merged_out(3)
     direct_out(4)

time: 90.3 us -> 90.1 us (level)
  no operation moved by 1% of the time
where the time goes in v7:
time: 90.1 us; the launch traced here: 90 us
  Pallas kernels  89.1 us (99%)
  local copies, waits for them, and re-layouts  0.97 us (1%)
    pallas_call x1, Pallas kernels, per_device(): pl.pallas_call(kernel, out_shape=pltpu.VMEM((NB * BLK, FEAT), BF16), in_s...  89.1 us

profile of v7, /device:TPU:1, one launch (start us, length us, event | category | flops | bytes accessed | tf_op | source)
XLA Modules:
  0.0 90.0 jit_solution(4481806610936167392)
XLA Ops:
  0.0 89.1 %shard_map.64 = bf16[512,1024]{1,0:T(8,128)(2,1)S(1)} custom-call(s32[4]{0:T(128)} %ids.1, bf16[512,1024]{1,0:T(8,128)(2,1)} %tok.1, bf16[4096,512]{1,0:T(8,128)(2,1)} %wq.1, bf16[4096,512]{1,0:T(8,128)(2,1)} %wk.1, bf16[4096,512]{1,0:T(8,128)(2,1)} %wv.1, bf16[512,4096]{1,0:T(8,128)(2,1)} %wo.1), custom_call_target="tpu_custom_call" | custom-call | tf_op jit(solution)/shard_map/pallas_call | solution.py:473
  89.1 1.0 %copy.8 = bf16[512,1024]{1,0:T(8,128)(2,1)} copy(bf16[512,1024]{1,0:T(8,128)(2,1)S(1)} %shard_map.64) | data formatting | bytes 2097152
